TPU v7x, 512 devices: a whole 4x8x8 slice. The times are simulated.
512 devices in a mesh: gx: 64 (over y, x, core), gy: 8 (over z).
Axes of the slice: x: 4, y: 8, z: 8, core: 2. Of those that a mesh axis runs over, the one named last changes fastest.
Arguments:
- residual: float32 [64, 256, 2048], P(None, 'gx', 'gy'), may hold values from -6 to 6
- classes: int32 [64, 256, 2048], P(None, 'gx', 'gy'), may hold values from 0 to 15
- class_perm: float32 [16], replicated, may hold values from 0.1 to 10
- support: int32 [64, 256, 2048], P(None, 'gx', 'gy'), may hold values from 0 to 15
- coarse_inverse: float32 [8192, 8192], P(('gx', 'gy')), may hold values from -0.00020716019 to 0.0071875
Outputs:
- preconditioned: float32 [64, 256, 2048], P(None, 'gx', 'gy')
All inputs are finite; a program needn't handle non-finite values.
Results may differ from a plain program's by a relative error of at most 0.0003.
Values sent between devices are 32-bit elements; how exact they have to be, the bound alone decides.
No kernel may reach another device: no remote copies, remote signals or barrier semaphores. Data moves between devices by JAX's collectives and lax.ppermute only.
A program may use at most 64 MiB of HBM per device.

v0:
```python
import jax
import jax.numpy as jnp
from jax import lax
from jax.sharding import PartitionSpec as P

SWEEPS = 4


lower_bound = 0.1
upper_bound = 2.0


def padded_2(block, sides, width):
    for axis, dim in sides:
        count = lax.axis_size(axis)
        forward = [(i, i + 1) for i in range(count - 1)]
        backward = [(target, source) for source, target in forward]
        low = lax.ppermute(
            lax.slice_in_dim(block, block.shape[dim] - width, None, axis=dim), axis, forward
        )
        high = lax.ppermute(lax.slice_in_dim(block, 0, width, axis=dim), axis, backward)
        block = jnp.concatenate([low, block, high], axis=dim)
    return block


def neighbours():
    return [(0, -1), (0, 1), (1, -1), (1, 1), (2, -1), (2, 1)]


def shifted(padded, along, offset):
    window = [slice(1, -1), slice(1, -1), slice(1, -1)]
    window[along] = slice(1 + offset, padded.shape[along] - 1 + offset)
    return padded[tuple(window)]


def couplings(perm_pad, inside_pad):
    center = shifted(perm_pad, 0, 0)
    links = []
    for along, offset in neighbours():
        beside = shifted(perm_pad, along, offset)
        beside_in = shifted(inside_pad, along, offset) > 0
        harmonic = 2.0 * center * beside / (center + jnp.where(beside_in, beside, 1.0))
        links.append(jnp.where(beside_in, harmonic, 2.0 * center))
    return links


def operate(padded, links, diagonal):
    summed = diagonal * shifted(padded, 0, 0)
    for link, pair in zip(links, neighbours()):
        summed = summed - link * shifted(padded, pair[0], pair[1])
    return summed


def chebyshev(source, links, diagonal, extend):
    middle = 0.5 * (upper_bound + lower_bound)
    spread = 0.5 * (upper_bound - lower_bound)
    sigma_ratio = middle / spread
    weight_old = 1.0 / sigma_ratio
    inverse_diag = 1.0 / diagonal
    update = inverse_diag * source / middle
    smooth = update
    remain = source
    for sweep in range(SWEEPS - 1):
        remain = remain - operate(extend(update), links, diagonal)
        weight_new = 1.0 / (2.0 * sigma_ratio - weight_old)
        update = (
            weight_new * weight_old * update + 2.0 * weight_new / spread * inverse_diag * remain
        )
        smooth = smooth + update
        weight_old = weight_new
    return smooth


def inside_mask(count_x, count_y, offset, height, width_x, width_y):
    x_glob = lax.axis_index("gx") * width_x - offset + jnp.arange(count_x)
    y_glob = lax.axis_index("gy") * width_y - offset + jnp.arange(count_y)
    x_inside = (x_glob >= 0) & (x_glob < width_x * lax.axis_size("gx"))
    y_inside = (y_glob >= 0) & (y_glob < width_y * lax.axis_size("gy"))
    z_levels = jnp.arange(height)
    z_inside = (z_levels >= 1) & (z_levels <= height - 2)
    joined = z_inside[:, None, None] & x_inside[None, :, None] & y_inside[None, None, :]
    return joined.astype(jnp.float32)


def exchange_rim(field):
    grown = padded_2(field, (("gx", 1), ("gy", 2)), 1)
    return jnp.pad(grown, ((1, 1), (0, 0), (0, 0)))


def local(residual, classes, class_perm, support, coarse_inverse):
    depth_z, width_x, width_y = residual.shape
    functions = coarse_inverse.shape[0]
    perm = jnp.zeros(residual.shape, jnp.float32)
    for c in range(class_perm.shape[0]):
        perm = perm + jnp.where(classes == c, class_perm[c], 0.0)
    coarse_local = jnp.stack(
        [jnp.sum(jnp.where(support == c, residual, 0.0)) for c in range(functions)]
    )
    gathered = lax.all_gather(coarse_local, ("gx", "gy"), axis=0, tiled=True)
    coarse_values = jnp.dot(coarse_inverse, gathered, precision=lax.Precision.HIGHEST)
    perm_grown = padded_2(perm, (("gx", 1), ("gy", 2)), 1)
    perm_pad = jnp.pad(perm_grown, ((1, 1), (0, 0), (0, 0)))
    inside_pad = inside_mask(width_x + 2, width_y + 2, 1, depth_z + 2, width_x, width_y)
    links = couplings(perm_pad, inside_pad)
    summed_links = links[0]
    for link in links[1:]:
        summed_links = summed_links + link
    inside_core = shifted(inside_pad, 0, 0) > 0
    diagonal = jnp.where(inside_core, summed_links, 1.0)
    smooth = chebyshev(residual, links, diagonal, exchange_rim)
    correction = jnp.zeros(residual.shape, jnp.float32)
    for c in range(functions):
        correction = correction + jnp.where(support == c, coarse_values[c], 0.0)
    return smooth + correction


def solution(mesh):
    return jax.shard_map(
        local,
        mesh=mesh,
        in_specs=(
            P(None, "gx", "gy"),
            P(None, "gx", "gy"),
            P(),
            P(None, "gx", "gy"),
            P(("gx", "gy"), None),
        ),
        out_specs=P(None, "gx", "gy"),
        check_vma=False,
    )
```

profile of v0, /device:TPU:1, one launch (start us, length us, event | category | flops | bytes accessed | tf_op | source)
XLA Modules:
  0.0 238.3 jit_solution(13737981022848986247)
XLA Ops:
  1.9 11.7 %select_add_fusion = f32[64,4,256]{2,1,0:T(4,128)S(1)} fusion(s32[64,4,256]{2,1,0:T(4,128)} %param.6, f32[]{:T(128)} %bitcast.15, f32[]{:T(128)} %bitcast.14, f32[]{:T(128)} %bitcast.13, f32[]{:T(128)} %bitcast.12, f32[]{:T(128)} %bitcast.11, f32[]{:T(128)} %bitcast.10, f32[]{:T(128)} %bitcast.9, f32[]{:T(128)} %bitcast.8, f32[]{:T(128)} %bitcast.7, ...), kind=kLoop, calls=%fused_computation.140 | loop fusion | flops 3080192 | bytes 524352 | tf_op jit(solution)/shard_map/add | solution.py:95
  13.7 4.5 %collective-permute-start = (f32[64,1,256]{2,1,0:T(1,128)S(1)}, f32[64,1,256]{2,1,0:T(1,128)S(1)}, u32[]{:S(2)}, u32[]{:S(2)}) collective-permute-start(f32[64,1,256]{2,1,0:T(1,128)S(1)} %get-tuple-element.64), channel_id=1, source_target_pairs={{0,8},{8,16},{16,24},{24,32},{32,40},{40,48},{48,56},{56,64},{64,7... | collective-permute-start | bytes 196616 | tf_op jit(solution)/shard_map/ppermute | solution.py:18
  18.3 5.6 %collective-permute-start.1 = (f32[64,1,256]{2,1,0:T(1,128)S(1)}, f32[64,1,256]{2,1,0:T(1,128)S(1)}, u32[]{:S(2)}, u32[]{:S(2)}) collective-permute-start(f32[64,1,256]{2,1,0:T(1,128)S(1)} %get-tuple-element.65), channel_id=1, source_target_pairs={{8,0},{16,8},{24,16},{32,24},{40,32},{48,40},{56,48},{64,56},{72,6... | collective-permute-start | bytes 196616 | tf_op jit(solution)/shard_map/ppermute | solution.py:21
  25.0 3.1 %collective-permute-start.2 = (f32[64,6,1]{2,1,0:T(8,128)S(1)}, f32[64,6,1]{2,1,0:T(8,128)S(1)}, u32[]{:S(2)}, u32[]{:S(2)}) collective-permute-start(f32[64,6,1]{2,1,0:T(8,128)S(1)} %get-tuple-element.56), channel_id=1, source_target_pairs={{0,1},{1,2},{2,3},{3,4},{4,5},{5,6},{6,7},{8,9},{9,10},{10,11},{11... | collective-permute-start | bytes 4616 | tf_op jit(solution)/shard_map/ppermute | solution.py:18
  29.6 3.3 %collective-permute-done.2 = f32[64,6,1]{2,1,0:T(8,128)S(1)} collective-permute-done((f32[64,6,1]{2,1,0:T(8,128)S(1)}, f32[64,6,1]{2,1,0:T(8,128)S(1)}, u32[]{:S(2)}, u32[]{:S(2)}) %collective-permute-start.2) | collective-permute-done | bytes 1568 | tf_op jit(solution)/shard_map/ppermute | solution.py:18
  33.0 4.1 %collective-permute-done.3 = f32[64,6,1]{2,1,0:T(8,128)S(1)} collective-permute-done((f32[64,6,1]{2,1,0:T(8,128)S(1)}, f32[64,6,1]{2,1,0:T(8,128)S(1)}, u32[]{:S(2)}, u32[]{:S(2)}) %collective-permute-start.3) | collective-permute-done | bytes 1568 | tf_op jit(solution)/shard_map/ppermute | solution.py:21
  37.9 2.6 %multiply_multiply_fusion.3 = (f32[64,4,256]{2,1,0:T(4,128)S(1)}, f32[64,4,256]{2,1,0:T(4,128)S(1)}, f32[64,4,256]{2,1,0:T(4,128)S(1)}, f32[64,4,256]{2,1,0:T(4,...) fusion(f32[64,4,256]{2,1,0:T(4,128)S(1)} %copy-done.1, ...), kind=kLoop, calls=%fused_computation.141 | loop fusion | flops 3604480 | bytes 5180416 | tf_op jit(solution)/shard_map/div | solution.py:60
  40.6 4.0 %collective-permute-start.4 = (f32[64,1,256]{2,1,0:T(1,128)S(1)}, f32[64,1,256]{2,1,0:T(1,128)S(1)}, u32[]{:S(2)}, u32[]{:S(2)}) collective-permute-start(f32[64,1,256]{2,1,0:T(1,128)S(1)} %get-tuple-element.62), channel_id=1, source_target_pairs={{0,8},{8,16},{16,24},{24,32},{32,40},{40,48},{48,56},{56,64},{64,7... | collective-permute-start | bytes 196616 | tf_op jit(solution)/shard_map/ppermute | solution.py:18
  46.6 3.6 %collective-permute-done.5 = f32[64,1,256]{2,1,0:T(1,128)S(1)} collective-permute-done((f32[64,1,256]{2,1,0:T(1,128)S(1)}, f32[64,1,256]{2,1,0:T(1,128)S(1)}, u32[]{:S(2)}, u32[]{:S(2)}) %collective-permute-start.5) | collective-permute-done | bytes 65568 | tf_op jit(solution)/shard_map/ppermute | solution.py:21
  50.6 4.0 %collective-permute-start.6 = (f32[64,6,1]{2,1,0:T(8,128)S(1)}, f32[64,6,1]{2,1,0:T(8,128)S(1)}, u32[]{:S(2)}, u32[]{:S(2)}) collective-permute-start(f32[64,6,1]{2,1,0:T(8,128)S(1)} %get-tuple-element.54), channel_id=1, source_target_pairs={{0,1},{1,2},{2,3},{3,4},{4,5},{5,6},{6,7},{8,9},{9,10},{10,11},{11... | collective-permute-start | bytes 4616 | tf_op jit(solution)/shard_map/ppermute | solution.py:18
  55.9 2.8 %collective-permute-done.6 = f32[64,6,1]{2,1,0:T(8,128)S(1)} collective-permute-done((f32[64,6,1]{2,1,0:T(8,128)S(1)}, f32[64,6,1]{2,1,0:T(8,128)S(1)}, u32[]{:S(2)}, u32[]{:S(2)}) %collective-permute-start.6) | collective-permute-done | bytes 1568 | tf_op jit(solution)/shard_map/ppermute | solution.py:18
  58.7 5.7 %collective-permute-done.7 = f32[64,6,1]{2,1,0:T(8,128)S(1)} collective-permute-done((f32[64,6,1]{2,1,0:T(8,128)S(1)}, f32[64,6,1]{2,1,0:T(8,128)S(1)}, u32[]{:S(2)}, u32[]{:S(2)}) %collective-permute-start.7) | collective-permute-done | bytes 1568 | tf_op jit(solution)/shard_map/ppermute | solution.py:21
  66.7 4.0 %collective-permute-start.8 = (f32[64,1,256]{2,1,0:T(1,128)S(1)}, f32[64,1,256]{2,1,0:T(1,128)S(1)}, u32[]{:S(2)}, u32[]{:S(2)}) collective-permute-start(f32[64,1,256]{2,1,0:T(1,128)S(1)} %get-tuple-element.60), channel_id=1, source_target_pairs={{0,8},{8,16},{16,24},{24,32},{32,40},{40,48},{48,56},{56,64},{64,7... | collective-permute-start | bytes 196616 | tf_op jit(solution)/shard_map/ppermute | solution.py:18
  72.6 3.7 %select_reduce_fusion = (f32[]{:T(128)}, f32[]{:T(128)}, f32[]{:T(128)}, f32[]{:T(128)}, f32[]{:T(128)}, /*index=5*/f32[]{:T(128)}, f32[]{:T(128)}, f32[]{:T(128...) fusion(f32[64,4,256]{2,1,0:T(4,128)S(1)} %copy-done.1, ...), kind=kLoop, calls=%fused_computation.107 | loop fusion | flops 3145712 | bytes 1572928 | tf_op jit(solution)/shard_map/reduce_sum | solution.py:97
  76.3 10.0 %stack.67 = f32[16]{0:T(128)S(1)} concatenate(f32[1]{0:T(128)} %bitcast.16, f32[1]{0:T(128)} %bitcast.17, f32[1]{0:T(128)} %bitcast.18, f32[1]{0:T(128)} %bitcast.19, f32[1]{0:T(128)} %bitcast.20, f32[1]{0:T(128)} %bitcast.21, f32[1]{0:T(128)} %bitcast.22, f32[1]{0:T(128)} %bitcast.23, f32[1]{0:T(128)} %bitcast.24, f32[1]{0:T(128)} %bitcast.25, f32[1]{0:T(128)} %bitcast.26, ...), dimensions={0} | concatenate | bytes 128 | tf_op jit(solution)/shard_map/stack | solution.py:96
  88.1 5.3 %collective-permute-start.10 = (f32[64,6,1]{2,1,0:T(8,128)}, f32[64,6,1]{2,1,0:T(8,128)S(1)}, u32[]{:S(2)}, u32[]{:S(2)}) collective-permute-start(f32[64,6,1]{2,1,0:T(8,128)} %get-tuple-element.52), channel_id=1, source_target_pairs={{0,1},{1,2},{2,3},{3,4},{4,5},{5,6},{6,7},{8,9},{9,10},{10,11},{11... | collective-permute-start | bytes 4616 | tf_op jit(solution)/shard_map/ppermute | solution.py:18
  94.7 102.7 %all-reduce.4 = f32[8192]{0:T(1024)} all-reduce(f32[8192]{0:T(1024)} %copy-done.22), channel_id=1, replica_groups=mesh['gx'=64,'gy'=8] {'gx','gy'}, use_global_device_ids=true, to_apply=%add.4 | all-reduce | flops 8192 | bytes 65536
  199.2 2.3 multiply_add_fusion
  201.7 4.2 %collective-permute-start.12 = (f32[64,1,256]{2,1,0:T(1,128)S(1)}, f32[64,1,256]{2,1,0:T(1,128)S(1)}, u32[]{:S(2)}, u32[]{:S(2)}) collective-permute-start(f32[64,1,256]{2,1,0:T(1,128)S(1)} %get-tuple-element.58), channel_id=1, source_target_pairs={{0,8},{8,16},{16,24},{24,32},{32,40},{40,48},{48,56},{56,64},{64,7... | collective-permute-start | bytes 196616 | tf_op jit(solution)/shard_map/ppermute | solution.py:18
  208.6 2.9 %collective-permute-done.13 = f32[64,1,256]{2,1,0:T(1,128)S(1)} collective-permute-done((f32[64,1,256]{2,1,0:T(1,128)S(1)}, f32[64,1,256]{2,1,0:T(1,128)S(1)}, u32[]{:S(2)}, u32[]{:S(2)}) %collective-permute-start.13) | collective-permute-done | bytes 65568 | tf_op jit(solution)/shard_map/ppermute | solution.py:21
  211.8 2.8 %collective-permute-start.14 = (f32[64,6,1]{2,1,0:T(8,128)S(1)}, f32[64,6,1]{2,1,0:T(8,128)S(1)}, u32[]{:S(2)}, u32[]{:S(2)}) collective-permute-start(f32[64,6,1]{2,1,0:T(8,128)S(1)} %get-tuple-element.50), channel_id=1, source_target_pairs={{0,1},{1,2},{2,3},{3,4},{4,5},{5,6},{6,7},{8,9},{9,10},{10,11},{11... | collective-permute-start | bytes 4616 | tf_op jit(solution)/shard_map/ppermute | solution.py:18
  216.6 2.1 collective-permute-done.14
  218.8 4.1 %collective-permute-done.15 = f32[64,6,1]{2,1,0:T(8,128)S(1)} collective-permute-done((f32[64,6,1]{2,1,0:T(8,128)S(1)}, f32[64,6,1]{2,1,0:T(8,128)S(1)}, u32[]{:S(2)}, u32[]{:S(2)}) %collective-permute-start.15) | collective-permute-done | bytes 1568 | tf_op jit(solution)/shard_map/ppermute | solution.py:21
  224.7 13.6 %fusion.7 = f32[64,4,256]{2,1,0:T(4,128)} fusion(f32[64,4,256]{2,1,0:T(4,128)S(1)} %get-tuple-element.38, f32[64,4,256]{2,1,0:T(4,128)S(1)} %get-tuple-element.49, f32[64,6,1]{2,1,0:T(8,128)S(1)} %collective-permute-done.15, f32[64,1,256]{2,1,0:T(1,128)S(1)} %collective-permute-done.13, f32[64,4,256]{2,1,0:T(4,128)S(1)} %get-tuple-element.37, ...), kind=kLoop, calls=%fused_computation.32 | loop fusion | flops 4784128 | bytes 4918336 | tf_op jit(solution)/shard_map/add | solution.py:114
  (88 shorter events, 24.8 us)
Async XLA Ops:
  0.0 207.8 %copy-start = (f32[16,8192]{1,0:T(8,128)S(1)}, f32[16,8192]{1,0:T(8,128)}, u32[]{:S(2)}) copy-start(f32[16,8192]{1,0:T(8,128)} %param.9) | copy-start | bytes 1572868
  13.7 10.2 %collective-permute-start = (f32[64,1,256]{2,1,0:T(1,128)S(1)}, f32[64,1,256]{2,1,0:T(1,128)S(1)}, u32[]{:S(2)}, u32[]{:S(2)}) collective-permute-start(f32[64,1,256]{2,1,0:T(1,128)S(1)} %get-tuple-element.64), channel_id=1, source_target_pairs={{0,8},{8,16},{16,24},{24,32},{32,40},{40,48},{48,56},{56,64},{64,7... | collective-permute-start | bytes 196616 | tf_op jit(solution)/shard_map/ppermute | solution.py:18
  18.3 6.5 %collective-permute-start.1 = (f32[64,1,256]{2,1,0:T(1,128)S(1)}, f32[64,1,256]{2,1,0:T(1,128)S(1)}, u32[]{:S(2)}, u32[]{:S(2)}) collective-permute-start(f32[64,1,256]{2,1,0:T(1,128)S(1)} %get-tuple-element.65), channel_id=1, source_target_pairs={{8,0},{16,8},{24,16},{32,24},{40,32},{48,40},{56,48},{64,56},{72,6... | collective-permute-start | bytes 196616 | tf_op jit(solution)/shard_map/ppermute | solution.py:21
  25.0 7.9 %collective-permute-start.2 = (f32[64,6,1]{2,1,0:T(8,128)S(1)}, f32[64,6,1]{2,1,0:T(8,128)S(1)}, u32[]{:S(2)}, u32[]{:S(2)}) collective-permute-start(f32[64,6,1]{2,1,0:T(8,128)S(1)} %get-tuple-element.56), channel_id=1, source_target_pairs={{0,1},{1,2},{2,3},{3,4},{4,5},{5,6},{6,7},{8,9},{9,10},{10,11},{11... | collective-permute-start | bytes 4616 | tf_op jit(solution)/shard_map/ppermute | solution.py:18
  28.2 8.9 %collective-permute-start.3 = (f32[64,6,1]{2,1,0:T(8,128)S(1)}, f32[64,6,1]{2,1,0:T(8,128)S(1)}, u32[]{:S(2)}, u32[]{:S(2)}) collective-permute-start(f32[64,6,1]{2,1,0:T(8,128)S(1)} %get-tuple-element.57), channel_id=1, source_target_pairs={{1,0},{2,1},{3,2},{4,3},{5,4},{6,5},{7,6},{9,8},{10,9},{11,10},{12... | collective-permute-start | bytes 4616 | tf_op jit(solution)/shard_map/ppermute | solution.py:21
  29.6 8.3 %copy-start.1 = (f32[64,4,256]{2,1,0:T(4,128)S(1)}, f32[64,4,256]{2,1,0:T(4,128)}, u32[]{:S(2)}) copy-start(f32[64,4,256]{2,1,0:T(4,128)} %param.5) | copy-start | bytes 786436
  40.6 6.0 %collective-permute-start.4 = (f32[64,1,256]{2,1,0:T(1,128)S(1)}, f32[64,1,256]{2,1,0:T(1,128)S(1)}, u32[]{:S(2)}, u32[]{:S(2)}) collective-permute-start(f32[64,1,256]{2,1,0:T(1,128)S(1)} %get-tuple-element.62), channel_id=1, source_target_pairs={{0,8},{8,16},{16,24},{24,32},{32,40},{40,48},{48,56},{56,64},{64,7... | collective-permute-start | bytes 196616 | tf_op jit(solution)/shard_map/ppermute | solution.py:18
  44.7 5.6 %collective-permute-start.5 = (f32[64,1,256]{2,1,0:T(1,128)S(1)}, f32[64,1,256]{2,1,0:T(1,128)S(1)}, u32[]{:S(2)}, u32[]{:S(2)}) collective-permute-start(f32[64,1,256]{2,1,0:T(1,128)S(1)} %get-tuple-element.63), channel_id=1, source_target_pairs={{8,0},{16,8},{24,16},{32,24},{40,32},{48,40},{56,48},{64,56},{72,6... | collective-permute-start | bytes 196616 | tf_op jit(solution)/shard_map/ppermute | solution.py:21
  50.6 8.1 %collective-permute-start.6 = (f32[64,6,1]{2,1,0:T(8,128)S(1)}, f32[64,6,1]{2,1,0:T(8,128)S(1)}, u32[]{:S(2)}, u32[]{:S(2)}) collective-permute-start(f32[64,6,1]{2,1,0:T(8,128)S(1)} %get-tuple-element.54), channel_id=1, source_target_pairs={{0,1},{1,2},{2,3},{3,4},{4,5},{5,6},{6,7},{8,9},{9,10},{10,11},{11... | collective-permute-start | bytes 4616 | tf_op jit(solution)/shard_map/ppermute | solution.py:18
  54.6 9.8 %collective-permute-start.7 = (f32[64,6,1]{2,1,0:T(8,128)S(1)}, f32[64,6,1]{2,1,0:T(8,128)S(1)}, u32[]{:S(2)}, u32[]{:S(2)}) collective-permute-start(f32[64,6,1]{2,1,0:T(8,128)S(1)} %get-tuple-element.55), channel_id=1, source_target_pairs={{1,0},{2,1},{3,2},{4,3},{5,4},{6,5},{7,6},{9,8},{10,9},{11,10},{12... | collective-permute-start | bytes 4616 | tf_op jit(solution)/shard_map/ppermute | solution.py:21
  66.6 6.0 %copy-start.20 = (s32[64,4,256]{2,1,0:T(4,128)S(1)}, s32[64,4,256]{2,1,0:T(4,128)}, u32[]{:S(2)}) copy-start(s32[64,4,256]{2,1,0:T(4,128)} %param.8) | copy-start | bytes 786436
  66.7 19.9 %collective-permute-start.8 = (f32[64,1,256]{2,1,0:T(1,128)S(1)}, f32[64,1,256]{2,1,0:T(1,128)S(1)}, u32[]{:S(2)}, u32[]{:S(2)}) collective-permute-start(f32[64,1,256]{2,1,0:T(1,128)S(1)} %get-tuple-element.60), channel_id=1, source_target_pairs={{0,8},{8,16},{16,24},{24,32},{32,40},{40,48},{48,56},{56,64},{64,7... | collective-permute-start | bytes 196616 | tf_op jit(solution)/shard_map/ppermute | solution.py:18
  70.7 15.9 %collective-permute-start.9 = (f32[64,1,256]{2,1,0:T(1,128)S(1)}, f32[64,1,256]{2,1,0:T(1,128)S(1)}, u32[]{:S(2)}, u32[]{:S(2)}) collective-permute-start(f32[64,1,256]{2,1,0:T(1,128)S(1)} %get-tuple-element.61), channel_id=1, source_target_pairs={{8,0},{16,8},{24,16},{32,24},{40,32},{48,40},{56,48},{64,56},{72,6... | collective-permute-start | bytes 196616 | tf_op jit(solution)/shard_map/ppermute | solution.py:21
  88.1 109.3 %collective-permute-start.10 = (f32[64,6,1]{2,1,0:T(8,128)}, f32[64,6,1]{2,1,0:T(8,128)S(1)}, u32[]{:S(2)}, u32[]{:S(2)}) collective-permute-start(f32[64,6,1]{2,1,0:T(8,128)} %get-tuple-element.52), channel_id=1, source_target_pairs={{0,1},{1,2},{2,3},{3,4},{4,5},{5,6},{6,7},{8,9},{9,10},{10,11},{11... | collective-permute-start | bytes 4616 | tf_op jit(solution)/shard_map/ppermute | solution.py:18
  93.4 104.0 %collective-permute-start.11 = (f32[64,6,1]{2,1,0:T(8,128)}, f32[64,6,1]{2,1,0:T(8,128)}, u32[]{:S(2)}, u32[]{:S(2)}) collective-permute-start(f32[64,6,1]{2,1,0:T(8,128)} %get-tuple-element.53), channel_id=1, source_target_pairs={{1,0},{2,1},{3,2},{4,3},{5,4},{6,5},{7,6},{9,8},{10,9},{11,10},{12... | collective-permute-start | bytes 4616 | tf_op jit(solution)/shard_map/ppermute | solution.py:21
  197.4 1.8 copy-start.3
  201.6 6.3 %copy-start.21 = (f32[8192]{0:T(1024)S(1)}, f32[8192]{0:T(1024)}, u32[]{:S(2)}) copy-start(f32[8192]{0:T(1024)} %all-reduce.4) | copy-start | bytes 98308
  201.7 6.9 %collective-permute-start.12 = (f32[64,1,256]{2,1,0:T(1,128)S(1)}, f32[64,1,256]{2,1,0:T(1,128)S(1)}, u32[]{:S(2)}, u32[]{:S(2)}) collective-permute-start(f32[64,1,256]{2,1,0:T(1,128)S(1)} %get-tuple-element.58), channel_id=1, source_target_pairs={{0,8},{8,16},{16,24},{24,32},{32,40},{40,48},{48,56},{56,64},{64,7... | collective-permute-start | bytes 196616 | tf_op jit(solution)/shard_map/ppermute | solution.py:18
  205.9 5.6 %collective-permute-start.13 = (f32[64,1,256]{2,1,0:T(1,128)S(1)}, f32[64,1,256]{2,1,0:T(1,128)S(1)}, u32[]{:S(2)}, u32[]{:S(2)}) collective-permute-start(f32[64,1,256]{2,1,0:T(1,128)S(1)} %get-tuple-element.59), channel_id=1, source_target_pairs={{8,0},{16,8},{24,16},{32,24},{40,32},{48,40},{56,48},{64,56},{72,6... | collective-permute-start | bytes 196616 | tf_op jit(solution)/shard_map/ppermute | solution.py:21
  211.8 6.9 %collective-permute-start.14 = (f32[64,6,1]{2,1,0:T(8,128)S(1)}, f32[64,6,1]{2,1,0:T(8,128)S(1)}, u32[]{:S(2)}, u32[]{:S(2)}) collective-permute-start(f32[64,6,1]{2,1,0:T(8,128)S(1)} %get-tuple-element.50), channel_id=1, source_target_pairs={{0,1},{1,2},{2,3},{3,4},{4,5},{5,6},{6,7},{8,9},{9,10},{10,11},{11... | collective-permute-start | bytes 4616 | tf_op jit(solution)/shard_map/ppermute | solution.py:18
  214.6 8.2 %collective-permute-start.15 = (f32[64,6,1]{2,1,0:T(8,128)S(1)}, f32[64,6,1]{2,1,0:T(8,128)S(1)}, u32[]{:S(2)}, u32[]{:S(2)}) collective-permute-start(f32[64,6,1]{2,1,0:T(8,128)S(1)} %get-tuple-element.51), channel_id=1, source_target_pairs={{1,0},{2,1},{3,2},{4,3},{5,4},{6,5},{7,6},{9,8},{10,9},{11,10},{12... | collective-permute-start | bytes 4616 | tf_op jit(solution)/shard_map/ppermute | solution.py:21
  223.0 1.1 copy-start.17
  223.0 1.1 copy-start.18
  223.0 1.1 copy-start.19
  (15 other events, 14.2 us)
where the time goes:
time: 241 us; the launch traced here: 238 us
  blocking collectives  103 us (43%)
  starting transfers between devices  48.5 us (20%)
  other arithmetic  40.4 us (17%)
  waiting for transfers between devices  29.5 us (12%)
  local copies, waits for them, and re-layouts  15.9 us (7%)
    unnamed x1, blocking collectives  103 us
    ppermute x8, starting transfers between devices, padded_2(): lax.ppermute(lax.slice_in_dim(block, block.shape[dim] - width, None, axis...  32 us
    ppermute x8, waiting for transfers between devices, padded_2(): lax.ppermute(lax.slice_in_dim(block, 0, width, axis=dim), axis, backward)  21.2 us
    ppermute x8, starting transfers between devices, padded_2(): lax.ppermute(lax.slice_in_dim(block, 0, width, axis=dim), axis, backward)  16.5 us
    add x1, other arithmetic, local(): return smooth + correction  13.6 us
    add x1, other arithmetic, local(): perm = perm + jnp.where(classes == c, class_perm[c], 0.0)  11.7 us
    another operation x1, local copies, waits for them, and re-layouts, local(): jnp.stack([jnp.sum(jnp.where(support == c, residual, 0.0)) for c in range...  10 us
    ppermute x8, waiting for transfers between devices, padded_2(): lax.ppermute(lax.slice_in_dim(block, block.shape[dim] - width, None, axis...  8.29 us
  transfers between devices with their start and end apart: 16, of which 9 were waited for; matrix products, arithmetic and copies ran while one was open for 7% of the time, Pallas kernels for 0%

commit v1 on v0

v1 whole, which is shorter than its diff:
```python
import functools

import jax
import jax.numpy as jnp
from jax import lax
from jax.experimental import pallas as pl
from jax.experimental.pallas import tpu as pltpu
from jax.sharding import PartitionSpec as P

SWEEPS = 4
LOWER, UPPER = 0.1, 2.0
CF = 16
NZ, CX, LANES = 64, 4, 128
TILES = 2
ROWS = NZ * CX * TILES
STEP = CX * TILES
DEPTH = 4
WIDE = CX + 2 * DEPTH


def iota(shape, dim):
    return lax.broadcasted_iota(jnp.int32, shape, dim)


def inverse(value):
    guess = pl.reciprocal(value, approx=True)
    return guess * (2.0 - value * guess)


def rows_of(block):
    split = block.reshape(NZ, CX, TILES, LANES)
    return split.transpose(0, 2, 1, 3).reshape(ROWS, LANES)


def block_of(rows):
    split = rows.reshape(NZ, TILES, CX, LANES)
    return split.transpose(0, 2, 1, 3).reshape(NZ, CX, TILES * LANES)


def lane_table(entry, count):
    lane = iota((8, LANES), 1)
    table = jnp.zeros((8, LANES), jnp.float32)
    for c in range(count):
        table = jnp.where(lane == c, entry(c), table)
    return table


def pick(table, index):
    return jnp.take_along_axis(table, index, axis=1, mode="promise_in_bounds")


def column_to_lanes(column, first):
    place = iota((CF, LANES), 1) == iota((CF, LANES), 0) + first
    return jnp.sum(jnp.where(place, column, 0.0), axis=0, keepdims=True)


def coarse_kernel(residual_ref, support_ref, message_ref):
    def step(i, sums):
        at = pl.ds(pl.multiple_of(i * 8, 8), 8)
        value, which = residual_ref[at, :], support_ref[at, :]
        return tuple(s + jnp.where(which == c, value, 0.0) for c, s in enumerate(sums))

    zero = jnp.zeros((8, LANES), jnp.float32)
    sums = lax.fori_loop(0, ROWS // 8, step, (zero,) * CF, unroll=4)
    rows = jnp.concatenate([jnp.sum(s, axis=0, keepdims=True) for s in sums], axis=0)
    column = jnp.sum(rows, axis=1, keepdims=True)
    row = column_to_lanes(column, lax.axis_index("gy") * CF)
    message_ref[...] = jnp.broadcast_to(row[None], message_ref.shape)


def pack_kernel(perm_ref, residual_ref, classes_ref, payload_ref, edge_ref):
    table = lane_table(lambda c: 1.0 / jnp.full((8, LANES), perm_ref[c]), perm_ref.shape[0])

    def step(i, carry):
        at = pl.ds(pl.multiple_of(i * 8, 8), 8)
        payload_ref[at, :] = pick(table, classes_ref[at, :])
        payload_ref[pl.ds(pl.multiple_of(ROWS + i * 8, 8), 8), :] = residual_ref[at, :]
        return carry

    lax.fori_loop(0, ROWS // 8, step, 0, unroll=8)
    lane = iota((NZ, LANES), 1)
    edge = jnp.zeros((NZ, LANES), jnp.float32)
    for item in range(2 * CX):
        first = (item // CX) * ROWS + item % CX
        low = payload_ref[pl.ds(first, NZ, stride=STEP), :]
        high = payload_ref[pl.ds(first + CX, NZ, stride=STEP), :]
        both = jnp.where(lane < 64, low, high)
        if item:
            both = pltpu.roll(both, 8 * item, 1)
        edge = jnp.where((lane + 4) % LANES // 8 == item, both, edge)
    edge_ref[...] = edge


def merge_kernel(payload_ref, above_ref, below_ref, out_ref, sem):
    copy = pltpu.make_async_copy(payload_ref, out_ref.at[pl.ds(0, 2 * ROWS), :], sem)
    copy.start()
    lane = iota((NZ, LANES), 1)
    out_ref[pl.ds(2 * ROWS, NZ), :] = jnp.where(lane % 8 < 4, above_ref[...], below_ref[...])
    copy.wait()


def smooth_kernel(low_ref, own_ref, high_ref, out_ref, res, upd, rem, inv, tx, ty, tz, tzb, flux, total):
    middle = 0.5 * (UPPER + LOWER)
    spread = 0.5 * (UPPER - LOWER)
    sigma = middle / spread
    lane = iota((NZ, LANES), 1)
    row = iota((NZ, LANES), 0)
    halo = (lane < 4) | (lane >= LANES - 4)

    for part, ref in enumerate((low_ref, own_ref, high_ref)):
        edge = ref[pl.ds(2 * ROWS, NZ), :]
        for x in range(CX):
            i = part * CX + x
            for t in range(TILES):
                res[i, t] = ref[pl.ds(t * CX + x, NZ, stride=STEP), :]
                rem[i, t] = ref[pl.ds(ROWS + t * CX + x, NZ, stride=STEP), :]
            for item, plane in ((x, res), (CX + x, rem)):
                moved = pltpu.roll(edge, (LANES - 8 * item) % LANES, 1) if item else edge
                plane[i, TILES] = jnp.where(halo, moved, 0.0)

    def link(a, b):
        return 2.0 * inverse(jnp.maximum(a + b, 1e-3))

    def right(values):
        rolled = [pltpu.roll(v, LANES - 1, 1) for v in values]
        n = len(values)
        return [jnp.where(lane == LANES - 1, rolled[(t + 1) % n], rolled[t]) for t in range(n)]

    def left(values, count):
        rolled = [pltpu.roll(v, 1, 1) for v in values]
        return [jnp.where(lane == 0, rolled[t - 1], rolled[t]) for t in range(count)]

    def down(value):
        return jnp.where(row == NZ - 1, 0.0, pltpu.roll(value, NZ - 1, 0))

    def up(value, first):
        rolled = pltpu.roll(value, 1, 0)
        top = jnp.where(row[:8] == 0, first, rolled[:8])
        return jnp.concatenate([top, rolled[8:]], axis=0)

    tiles = range(TILES + 1)
    for t in tiles:
        tx[0, t] = link(res[0, t], res[1, t])

    def setup(i, carry):
        r = [res[i, t] for t in tiles]
        r_right = right(r)
        ly = [link(r[t], r_right[t]) for t in tiles]
        ly_left = left(ly, TILES + 1)
        for t in tiles:
            lx = link(r[t], res[i + 1, t])
            lz = link(r[t], down(r[t]))
            first = link(r[t][:8], 0.0)
            diagonal = lx + tx[i - 1, t] + ly[t] + ly_left[t] + lz + up(lz, first)
            inv_diag = jnp.where(r[t] > 0.0, inverse(diagonal), 0.0)
            tx[i, t], ty[i, t], tz[i, t], tzb[i, t] = lx, ly[t], lz, first
            inv[i, t] = inv_diag
            update = inv_diag * rem[i, t] * (1.0 / middle)
            upd[i, t] = update
            if t < TILES:
                total[i, t] = update
        return carry

    lax.fori_loop(1, WIDE - 1, setup, 0)

    weight_old = 1.0 / sigma
    for sweep in range(1, SWEEPS):
        last = sweep == SWEEPS - 1
        begin, end = 1 + sweep, WIDE - 1 - sweep
        weight_new = 1.0 / (2.0 * sigma - weight_old)
        keep, gain = weight_new * weight_old, 2.0 * weight_new / spread
        weight_old = weight_new
        done = range(TILES) if last else tiles
        for t in done:
            flux[t] = tx[begin - 1, t] * (upd[begin - 1, t] - upd[begin, t])

        def step(i, carry):
            u = [upd[i, t] for t in tiles]
            u_right = right(u)
            fy = [ty[i, t] * (u[t] - u_right[t]) for t in tiles]
            fy_left = left(fy, len(done))
            for t in done:
                fx = tx[i, t] * (u[t] - upd[i + 1, t])
                fz = tz[i, t] * (u[t] - down(u[t]))
                applied = fx - flux[t] + (fy[t] - fy_left[t]) + (fz - up(fz, -tzb[i, t] * u[t][:8]))
                flux[t] = fx
                remain = rem[i, t] - applied
                new = keep * u[t] + gain * inv[i, t] * remain
                if last:
                    out_ref[pl.ds(t * CX + i - DEPTH, NZ, stride=STEP), :] = total[i, t] + new
                else:
                    rem[i, t] = remain
                    upd[i, t] = new
                    if t < TILES:
                        total[i, t] = total[i, t] + new
            return carry

        lax.fori_loop(begin, end, step, 0)


def correct_kernel(gathered_ref, inverse_ref, support_ref, smooth_ref, out_ref):
    zero = jnp.zeros((CF, LANES), jnp.float32)
    sums = [zero] * 4
    count = gathered_ref.shape[0]
    for q in range(count):
        part = inverse_ref[:, q * LANES : (q + 1) * LANES] * gathered_ref[pl.ds(q, 1), :]
        sums[q % 4] = sums[q % 4] + part
    column = jnp.sum((sums[0] + sums[1]) + (sums[2] + sums[3]), axis=1, keepdims=True)
    table = jnp.broadcast_to(column_to_lanes(column, 0), (8, LANES))

    def step(i, carry):
        at = pl.ds(pl.multiple_of(i * 8, 8), 8)
        out_ref[at, :] = smooth_ref[at, :] + pick(table, support_ref[at, :])
        return carry

    lax.fori_loop(0, ROWS // 8, step, 0, unroll=8)


def vmem(count):
    return [pl.BlockSpec(memory_space=pltpu.VMEM)] * count


def call(kernel, outs, ins, args, scratch=(), flops=0, name=None):
    size = sum(a.size * 4 for a in args) + sum(o.size * 4 for o in outs)
    return pl.pallas_call(
        kernel,
        out_shape=outs,
        in_specs=ins,
        out_specs=vmem(len(outs)),
        scratch_shapes=scratch,
        compiler_params=pltpu.CompilerParams(vmem_limit_bytes=24 * 1024 * 1024),
        cost_estimate=pl.CostEstimate(flops=flops, bytes_accessed=size, transcendentals=0),
        name=name,
    )(*args)


def floats(*shape):
    return jax.ShapeDtypeStruct(shape, jnp.float32)


def spread_over(row, axis, groups=None):
    size = lax.axis_size(axis) if groups is None else len(groups[0])
    copies = jnp.broadcast_to(row[None], (size,) + row.shape)
    return lax.all_to_all(copies, axis, 0, 0, axis_index_groups=groups, tiled=True)


def local(residual, classes, class_perm, support, coarse_inverse):
    n_gx, n_gy = lax.axis_size("gx"), lax.axis_size("gy")
    near = LANES // CF
    residual, classes, support = rows_of(residual), rows_of(classes), rows_of(support)

    (message,) = call(
        coarse_kernel, [floats(n_gy, 1, LANES)], vmem(2), [residual, support], name="coarse"
    )
    payload, edge = call(
        pack_kernel,
        [floats(2 * ROWS, LANES), floats(NZ, LANES)],
        [pl.BlockSpec(memory_space=pltpu.SMEM)] + vmem(2),
        [class_perm, residual, classes],
        name="pack",
    )

    across = [[s * near + i for i in range(near)] for s in range(n_gx // near)]
    along = [[s * near + i for s in range(n_gx // near)] for i in range(near)]
    got = lax.all_to_all(message, "gy", 0, 0, tiled=True)
    row = jnp.sum(got, axis=0)
    got = spread_over(row, "gx", across).reshape(near, LANES)
    gathered = spread_over(got, "gx", along).reshape(n_gx, LANES)

    forward_y = [(i, i + 1) for i in range(n_gy - 1)]
    backward_y = [(j, i) for i, j in forward_y]
    forward_x = [(i, i + 1) for i in range(n_gx - 1)]
    backward_x = [(j, i) for i, j in forward_x]
    above = lax.ppermute(edge, "gy", backward_y)
    below = lax.ppermute(edge, "gy", forward_y)
    (own,) = call(
        merge_kernel,
        [floats(2 * ROWS + NZ, LANES)],
        vmem(3),
        [payload, above, below],
        scratch=[pltpu.SemaphoreType.DMA],
        name="merge",
    )
    low = lax.ppermute(own, "gx", forward_x)
    high = lax.ppermute(own, "gx", backward_x)
    planes = pltpu.VMEM((WIDE, TILES + 1, NZ, LANES), jnp.float32)
    (smooth,) = call(
        smooth_kernel,
        [floats(ROWS, LANES)],
        vmem(3),
        [low, own, high],
        scratch=[planes] * 7
        + [
            pltpu.VMEM((WIDE, TILES + 1, 8, LANES), jnp.float32),
            pltpu.VMEM((TILES + 1, NZ, LANES), jnp.float32),
            pltpu.VMEM((WIDE, TILES, NZ, LANES), jnp.float32),
        ],
        flops=20_000_000,
        name="smooth",
    )
    (out,) = call(
        correct_kernel,
        [floats(ROWS, LANES)],
        vmem(4),
        [gathered, coarse_inverse, support, smooth],
        name="correct",
    )
    return block_of(out)


def solution(mesh):
    return jax.shard_map(
        local,
        mesh=mesh,
        in_specs=(
            P(None, "gx", "gy"),
            P(None, "gx", "gy"),
            P(),
            P(None, "gx", "gy"),
            P(("gx", "gy"), None),
        ),
        out_specs=P(None, "gx", "gy"),
        check_vma=False,
    )
```

time: 241 us -> 65.1 us (0.27)
  blocking collectives: 103 us -> 24.9 us
  other arithmetic: 40.4 us -> 0.03 us
  waiting for transfers between devices: 29.5 us -> 1.67 us
  starting transfers between devices: 48.5 us -> 25.1 us
  local copies, waits for them, and re-layouts: 15.9 us -> 3.19 us
  Pallas kernels: 0 us -> 9.78 us
    unnamed x1 -> x0, blocking collectives: 103 us -> none
    ppermute x16 -> x4, starting transfers between devices: 48.5 us -> 16.7 us  [the longest x1 5.46 us: local(): below = lax.ppermute(edge, 'gy', forward_y)]
    add x4 -> x0, other arithmetic: 29 us -> none  [the longest x1 13.6 us: local(): return smooth + correction]
    ppermute x16 -> x4, waiting for transfers between devices: 29.5 us -> 1 us  [the longest x1 0.99 us: local(): below = lax.ppermute(edge, 'gy', forward_y)]
    all_to_all x0 -> x2, blocking collectives: none -> 24.9 us  [the longest x1 14.2 us: local(): got = lax.all_to_all(message, 'gy', 0, 0, tiled=True)]
    another operation x1 -> x0, local copies, waits for them, and re-layouts: 10 us -> none  [local(): jnp.stack([jnp.sum(jnp.where(support == c, residual, 0.0)) for c in range...]
    pallas_call x0 -> x5, Pallas kernels: none -> 9.78 us  [call(): pl.pallas_call(kernel, out_shape=outs, in_specs=ins, out_specs=vmem(len(o...]
    all_to_all x0 -> x1, starting transfers between devices: none -> 8.4 us  [spread_over(): lax.all_to_all(copies, axis, 0, 0, axis_index_groups=groups, tiled=True)]
  transfers between devices with their start and end apart: 16 -> 5, of which waited for: 9 -> 2; matrix products, arithmetic and copies ran while one was open for 7% -> 1% of each run, Pallas kernels for 0% -> 10%
where the time goes in v1:
time: 65.1 us; the launch traced here: 64.7 us
  starting transfers between devices  25.1 us (39%)
  blocking collectives  24.9 us (38%)
  Pallas kernels  9.78 us (15%)
  local copies, waits for them, and re-layouts  3.19 us (5%)
  waiting for transfers between devices  1.67 us (3%)
    all_to_all x1, blocking collectives, local(): got = lax.all_to_all(message, 'gy', 0, 0, tiled=True)  14.2 us
    all_to_all x1, blocking collectives, spread_over(): lax.all_to_all(copies, axis, 0, 0, axis_index_groups=groups, tiled=True)  10.7 us
    pallas_call x5, Pallas kernels, call(): pl.pallas_call(kernel, out_shape=outs, in_specs=ins, out_specs=vmem(len(o...  9.78 us
    all_to_all x1, starting transfers between devices, spread_over(): lax.all_to_all(copies, axis, 0, 0, axis_index_groups=groups, tiled=True)  8.4 us
    ppermute x1, starting transfers between devices, local(): below = lax.ppermute(edge, 'gy', forward_y)  5.46 us
    ppermute x1, starting transfers between devices, local(): high = lax.ppermute(own, 'gx', backward_x)  5.24 us
    ppermute x1, starting transfers between devices, local(): low = lax.ppermute(own, 'gx', forward_x)  4.67 us
    unnamed x12, local copies, waits for them, and re-layouts  2.56 us
  transfers between devices with their start and end apart: 5, of which 2 were waited for; matrix products, arithmetic and copies ran while one was open for 1% of the time, Pallas kernels for 10%

profile of v1, /device:TPU:1, one launch (start us, length us, event | category | flops | bytes accessed | tf_op | source)
XLA Modules:
  0.0 64.7 jit_solution(4655265461121270260)
XLA Ops:
  0.0 0.7 %copy-done.5 = f32[16]{0:T(128)S(1)} copy-done((f32[16]{0:T(128)S(1)}, f32[16]{0:T(128)}, u32[]{:S(2)}) %copy-start.5) | copy-done | bytes 88
  0.7 0.9 %copy-done = f32[64,4,256]{2,1,0:T(4,128)S(1)} copy-done((f32[64,4,256]{2,1,0:T(4,128)S(1)}, f32[64,4,256]{2,1,0:T(4,128)}, u32[]{:S(2)}) %copy-start) | copy-done | bytes 262168
  1.6 0.9 %copy-done.4 = s32[64,4,256]{2,1,0:T(4,128)S(1)} copy-done((s32[64,4,256]{2,1,0:T(4,128)S(1)}, s32[64,4,256]{2,1,0:T(4,128)}, u32[]{:S(2)}) %copy-start.4) | copy-done | bytes 262168
  2.6 1.4 %pack.1 = (f32[1024,128]{1,0:T(8,128)S(1)}, f32[64,128]{1,0:T(8,128)S(1)}) custom-call(f32[16]{0:T(128)S(1)} %copy-done.5, f32[512,128]{1,0:T(8,128)S(1)} %bitcast.22, s32[512,128]{1,0:T(8,128)S(1)} %bitcast.26), custom_call_target="tpu_custom_call" | custom-call | bytes 1081408 | tf_op jit(solution)/shard_map/pack/pallas_call | solution.py:225
  4.0 1.3 %collective-permute-start = (f32[64,128]{1,0:T(8,128)S(1)}, f32[64,128]{1,0:T(8,128)S(1)}, u32[]{:S(2)}, u32[]{:S(2)}) collective-permute-start(f32[64,128]{1,0:T(8,128)S(1)} %get-tuple-element.8), channel_id=1, source_target_pairs={{1,0},{2,1},{3,2},{4,3},{5,4},{6,5},{7,6},{9,8},{10,9},{11,10},{12... | collective-permute-start | bytes 98312 | tf_op jit(solution)/shard_map/ppermute | solution.py:274
  5.3 5.5 %collective-permute-start.1 = (f32[64,128]{1,0:T(8,128)S(1)}, f32[64,128]{1,0:T(8,128)S(1)}, u32[]{:S(2)}, u32[]{:S(2)}) collective-permute-start(f32[64,128]{1,0:T(8,128)S(1)} %get-tuple-element.8), channel_id=1, source_target_pairs={{0,1},{1,2},{2,3},{3,4},{4,5},{5,6},{6,7},{8,9},{9,10},{10,11},{11... | collective-permute-start | bytes 98312 | tf_op jit(solution)/shard_map/ppermute | solution.py:275
  10.7 0.0 collective-permute-done.above_ref
  10.7 1.0 %collective-permute-done.1.below_ref = f32[64,128]{1,0:T(8,128)S(1)} collective-permute-done((f32[64,128]{1,0:T(8,128)S(1)}, f32[64,128]{1,0:T(8,128)S(1)}, u32[]{:S(2)}, u32[]{:S(2)}) %collective-permute-start.1) | collective-permute-done | bytes 32800 | tf_op jit(solution)/shard_map/ppermute | solution.py:275
  11.7 0.1 merge.1.own_ref
  11.8 4.7 %collective-permute-start.2 = (f32[1088,128]{1,0:T(8,128)S(1)}, f32[1088,128]{1,0:T(8,128)S(1)}, u32[]{:S(2)}, u32[]{:S(2)}) collective-permute-start(f32[1088,128]{1,0:T(8,128)S(1)} %merge.1.own_ref), channel_id=1, source_target_pairs={{0,8},{8,16},{16,24},{24,32},{32,40},{40,48},{48,56},{56,64},{64,7... | collective-permute-start | bytes 1671176 | tf_op jit(solution)/shard_map/ppermute | solution.py:284
  16.5 5.2 %collective-permute-start.3 = (f32[1088,128]{1,0:T(8,128)S(1)}, f32[1088,128]{1,0:T(8,128)S(1)}, u32[]{:S(2)}, u32[]{:S(2)}) collective-permute-start(f32[1088,128]{1,0:T(8,128)S(1)} %merge.1.own_ref), channel_id=1, source_target_pairs={{8,0},{16,8},{24,16},{32,24},{40,32},{48,40},{56,48},{64,56},{72,6... | collective-permute-start | bytes 1671176 | tf_op jit(solution)/shard_map/ppermute | solution.py:285
  21.7 0.0 copy-done.1
  21.7 0.0 copy-done.2
  21.7 0.6 coarse.1
  22.3 14.2 %all_to_all.15 = f32[8,1,128]{2,1,0:T(1,128)S(1)} all-to-all(f32[8,1,128]{2,1,0:T(1,128)S(1)} %coarse.1), channel_id=1, replica_groups=mesh['gx'=64,'gy'=8] {'gy'}, dimensions={0} | all-to-all | bytes 8192 | tf_op jit(solution)/shard_map/all_to_all | solution.py:265
  36.5 10.7 %all_to_all.16 = f32[8,1,128]{2,1,0:T(1,128)S(1)} all-to-all(f32[8,1,128]{2,1,0:T(1,128)S(1)} %broadcast_in_dim.6), channel_id=1, replica_groups={{0,8,16,24,32,40,48,56},{64,72,80,88,96,104,112,120},{128,136,144,152,1..., dimensions={0} | all-to-all | bytes 8192 | tf_op jit(solution)/shard_map/all_to_all | solution.py:244
  47.3 0.6 broadcast_in_dim.15
  47.9 8.4 %all-to-all-start.2 = ((f32[8,8,128]{2,1,0:T(8,128)}), f32[8,8,128]{2,1,0:T(8,128)S(1)}, u32[]{:S(2)}, u32[]{:S(2)}) async-start(f32[8,8,128]{2,1,0:T(8,128)} %broadcast_in_dim.15), calls=%async_computation.2 | async-start | bytes 65536 | tf_op jit(solution)/shard_map/all_to_all | solution.py:244
  56.3 0.0 collective-permute-done.2.low_ref
  56.3 0.0 collective-permute-done.3.high_ref
  56.3 6.2 %smooth.1.smooth_ref = f32[512,128]{1,0:T(8,128)S(1)} custom-call(f32[1088,128]{1,0:T(8,128)S(1)} %collective-permute-done.2.low_ref, f32[1088,128]{1,0:T(8,128)S(1)} %merge.1.own_ref, f32[1088,128]{1,0:T(8,128)S(1)} %collective-permute-done.3.high_ref), custom_call_target="tpu_custom_call" | custom-call | flops 20000000 | bytes 1933312 | tf_op jit(solution)/shard_map/smooth/pallas_call | solution.py:225
  62.5 0.7 %all-to-all-done.2 = f32[8,8,128]{2,1,0:T(8,128)S(1)} async-done(((f32[8,8,128]{2,1,0:T(8,128)}), f32[8,8,128]{2,1,0:T(8,128)S(1)}, u32[]{:S(2)}, u32[]{:S(2)}) %all-to-all-start.2) | async-done | bytes 32800 | tf_op jit(solution)/shard_map/all_to_all | solution.py:244
  63.2 0.0 copy-done.3
  63.2 1.6 %correct.1 = f32[512,128]{1,0:T(8,128)} custom-call(f32[64,128]{1,0:T(8,128)S(1)} %bitcast.27, f32[16,8192]{1,0:T(8,128)S(1)} %copy-done.3, s32[512,128]{1,0:T(8,128)S(1)} %bitcast.25, f32[512,128]{1,0:T(8,128)S(1)} %smooth.1.smooth_ref), custom_call_target="tpu_custom_call" | custom-call | bytes 1343488 | tf_op jit(solution)/shard_map/correct/pallas_call | solution.py:225
  (8 shorter events, 0.0 us)
Async XLA Ops:
  0.0 0.7 %copy-start.5 = (f32[16]{0:T(128)S(1)}, f32[16]{0:T(128)}, u32[]{:S(2)}) copy-start(f32[16]{0:T(128)} %perm_ref.1) | copy-start | bytes 196
  0.7 0.9 %copy-start = (f32[64,4,256]{2,1,0:T(4,128)S(1)}, f32[64,4,256]{2,1,0:T(4,128)}, u32[]{:S(2)}) copy-start(f32[64,4,256]{2,1,0:T(4,128)} %param.5) | copy-start | bytes 786436
  1.6 0.9 %copy-start.4 = (s32[64,4,256]{2,1,0:T(4,128)S(1)}, s32[64,4,256]{2,1,0:T(4,128)}, u32[]{:S(2)}) copy-start(s32[64,4,256]{2,1,0:T(4,128)} %param.6) | copy-start | bytes 786436
  4.0 6.8 %collective-permute-start = (f32[64,128]{1,0:T(8,128)S(1)}, f32[64,128]{1,0:T(8,128)S(1)}, u32[]{:S(2)}, u32[]{:S(2)}) collective-permute-start(f32[64,128]{1,0:T(8,128)S(1)} %get-tuple-element.8), channel_id=1, source_target_pairs={{1,0},{2,1},{3,2},{4,3},{5,4},{6,5},{7,6},{9,8},{10,9},{11,10},{12... | collective-permute-start | bytes 98312 | tf_op jit(solution)/shard_map/ppermute | solution.py:274
  5.3 6.5 %collective-permute-start.1 = (f32[64,128]{1,0:T(8,128)S(1)}, f32[64,128]{1,0:T(8,128)S(1)}, u32[]{:S(2)}, u32[]{:S(2)}) collective-permute-start(f32[64,128]{1,0:T(8,128)S(1)} %get-tuple-element.8), channel_id=1, source_target_pairs={{0,1},{1,2},{2,3},{3,4},{4,5},{5,6},{6,7},{8,9},{9,10},{10,11},{11... | collective-permute-start | bytes 98312 | tf_op jit(solution)/shard_map/ppermute | solution.py:275
  11.7 10.0 %copy-start.1 = (f32[64,4,256]{2,1,0:T(4,128)S(1)}, f32[64,4,256]{2,1,0:T(4,128)}, u32[]{:S(2)}) copy-start(f32[64,4,256]{2,1,0:T(4,128)} %param.5) | copy-start | bytes 786436
  11.7 10.0 %copy-start.2 = (s32[64,4,256]{2,1,0:T(4,128)S(1)}, s32[64,4,256]{2,1,0:T(4,128)}, u32[]{:S(2)}) copy-start(s32[64,4,256]{2,1,0:T(4,128)} %param.8) | copy-start | bytes 786436
  11.8 44.5 %collective-permute-start.2 = (f32[1088,128]{1,0:T(8,128)S(1)}, f32[1088,128]{1,0:T(8,128)S(1)}, u32[]{:S(2)}, u32[]{:S(2)}) collective-permute-start(f32[1088,128]{1,0:T(8,128)S(1)} %merge.1.own_ref), channel_id=1, source_target_pairs={{0,8},{8,16},{16,24},{24,32},{32,40},{40,48},{48,56},{56,64},{64,7... | collective-permute-start | bytes 1671176 | tf_op jit(solution)/shard_map/ppermute | solution.py:284
  16.5 39.8 %collective-permute-start.3 = (f32[1088,128]{1,0:T(8,128)S(1)}, f32[1088,128]{1,0:T(8,128)S(1)}, u32[]{:S(2)}, u32[]{:S(2)}) collective-permute-start(f32[1088,128]{1,0:T(8,128)S(1)} %merge.1.own_ref), channel_id=1, source_target_pairs={{8,0},{16,8},{24,16},{32,24},{40,32},{48,40},{56,48},{64,56},{72,6... | collective-permute-start | bytes 1671176 | tf_op jit(solution)/shard_map/ppermute | solution.py:285
  47.9 15.3 %all-to-all-start.2 = ((f32[8,8,128]{2,1,0:T(8,128)}), f32[8,8,128]{2,1,0:T(8,128)S(1)}, u32[]{:S(2)}, u32[]{:S(2)}) async-start(f32[8,8,128]{2,1,0:T(8,128)} %broadcast_in_dim.15), calls=%async_computation.2 | async-start | bytes 65536 | tf_op jit(solution)/shard_map/all_to_all | solution.py:244
  56.3 6.9 %copy-start.3 = (f32[16,8192]{1,0:T(8,128)S(1)}, f32[16,8192]{1,0:T(8,128)}, u32[]{:S(2)}) copy-start(f32[16,8192]{1,0:T(8,128)} %inverse_ref.1) | copy-start | bytes 1572868

commit v2 on v1

v2 whole, which is shorter than its diff:
```python
import math

import jax
import jax.numpy as jnp
from jax import lax
from jax.experimental import pallas as pl
from jax.experimental.pallas import tpu as pltpu
from jax.sharding import PartitionSpec as P

SWEEPS = 4
LOWER, UPPER = 0.1, 2.0
CF = 16
NZ, CX, LANES = 64, 4, 128
TILES = 2
ROWS = NZ * CX * TILES
STEP = CX * TILES
GROUPS = NZ // 8
FAR_ROW = 8 * STEP
DEPTH = 4
WIDE = CX + 2 * DEPTH
STRIP = 16
OWN = 2 * ROWS + 2 * STRIP
FACE = 8
CHUNKS = 4
FAR = 10**10
NOTHING = 1e-30


def iota(shape, dim):
    return lax.broadcasted_iota(jnp.int32, shape, dim)


def inverse(value):
    return pltpu.reciprocal(value, approx=True)


def rows_of(block):
    split = block.reshape(NZ, CX, TILES, LANES)
    return split.transpose(0, 2, 1, 3).reshape(ROWS, LANES)


def block_of(rows):
    split = rows.reshape(NZ, TILES, CX, LANES)
    return split.transpose(0, 2, 1, 3).reshape(NZ, CX, TILES * LANES)


def lane_table(entry, count):
    lane = iota((8, LANES), 1)
    table = jnp.zeros((8, LANES), jnp.float32)
    for c in range(count):
        table = jnp.where(lane == c, entry(c), table)
    return table


def pick(table, index):
    return jnp.take_along_axis(table, index, axis=1, mode="promise_in_bounds")


def column_to_lanes(column, first):
    place = iota((CF, LANES), 1) == iota((CF, LANES), 0) + first
    return jnp.sum(jnp.where(place, column, 0.0), axis=0, keepdims=True)


def vector(ref, base, t, x, j):
    return ref[pl.ds(base + j * STEP + t * CX + x, 8, stride=FAR_ROW), :]


def coarse_kernel(
    perm_ref, residual_ref, support_ref, classes_ref, message_ref, own_ref,
    support_buf, classes_buf, perm_buf, sems, perm_sem, classes_sem,
):
    size = ROWS // CHUNKS
    perm_copy = pltpu.make_async_copy(perm_ref, perm_buf, perm_sem)
    classes_copy = pltpu.make_async_copy(classes_ref, classes_buf, classes_sem)

    def copies(k):
        at = pl.ds(k * size, size)
        return [
            pltpu.make_async_copy(residual_ref.at[at, :], own_ref.at[pl.ds(ROWS + k * size, size), :], sems.at[k, 0]),
            pltpu.make_async_copy(support_ref.at[at, :], support_buf.at[at, :], sems.at[k, 1]),
        ]

    perm_copy.start()
    for k in range(CHUNKS):
        for copy in copies(k):
            copy.start()
    classes_copy.start()

    def add(i, sums):
        value = own_ref[pl.ds(pl.multiple_of(ROWS + i * 8, 8), 8), :]
        which = support_buf[pl.ds(pl.multiple_of(i * 8, 8), 8), :]
        return tuple(s + jnp.where(which == c, value, 0.0) for c, s in enumerate(sums))

    sums = (jnp.zeros((8, LANES), jnp.float32),) * CF
    for k in range(CHUNKS):
        for copy in copies(k):
            copy.wait()
        sums = lax.fori_loop(k * size // 8, (k + 1) * size // 8, add, sums, unroll=4)
    rows = jnp.concatenate([jnp.sum(s, axis=0, keepdims=True) for s in sums], axis=0)
    column = jnp.sum(rows, axis=1, keepdims=True)
    row = column_to_lanes(column, lax.axis_index("gy") * CF)

    perm_copy.wait()
    table = lane_table(lambda c: 1.0 / jnp.full((8, LANES), perm_buf[c]), perm_ref.shape[0])
    classes_copy.wait()

    def look_up(i, carry):
        at = pl.ds(pl.multiple_of(i * 8, 8), 8)
        own_ref[at, :] = pick(table, classes_buf[at, :])
        return carry

    lax.fori_loop(0, ROWS // 8, look_up, 0, unroll=8)

    lane = iota((8, LANES), 1)
    for h in range(2):
        first = jnp.zeros((8, LANES), jnp.float32)
        final = jnp.zeros((8, LANES), jnp.float32)
        for g in range(GROUPS // 2):
            for item in range(2 * CX):
                low, high = (vector(own_ref, item // CX * ROWS, t, item % CX, 2 * g + h) for t in range(2))
                both = jnp.where(lane < 64, low, high)
                shift = 32 * g + 4 * item
                if shift:
                    both = pltpu.roll(both, shift, 1)
                first = jnp.where(lane // 4 == shift // 4, both, first)
                final = jnp.where((lane + 4) % LANES // 4 == shift // 4, both, final)
        me = lax.axis_index("gy")
        for k in range(message_ref.shape[0]):
            message_ref[k, FACE + 8 * h : FACE + 8 * h + 8, :] = jnp.where(me < k, final, first)
    for k in range(message_ref.shape[0]):
        message_ref[k, 0:FACE, :] = jnp.broadcast_to(row, (FACE, LANES))


def merge_kernel(got_ref, own_ref, rows_ref, out_ref):
    count = got_ref.shape[0]
    row = got_ref[0, 0:1, :]
    for k in range(1, count):
        row = row + got_ref[k, 0:1, :]
    for k in range(rows_ref.shape[0]):
        rows_ref[k] = row
    me = lax.axis_index("gy")
    strip = pl.ds(FACE, STRIP)
    above = got_ref[jnp.minimum(me + 1, count - 1), strip, :]
    below = got_ref[jnp.maximum(me - 1, 0), strip, :]
    out_ref[pl.ds(2 * ROWS, STRIP), :] = jnp.where(me < count - 1, above, 0.0)
    out_ref[pl.ds(2 * ROWS + STRIP, STRIP), :] = jnp.where(me > 0, below, 0.0)


def fan_kernel(got_ref, copies_ref):
    for k in range(copies_ref.shape[0]):
        copies_ref[k] = got_ref[...]


def smooth_kernel(low_ref, own_ref, high_ref, after_ref, out_ref, res, upd, rem, inv, tx, ty, tz, tzu, flux, total):
    middle = 0.5 * (UPPER + LOWER)
    spread = 0.5 * (UPPER - LOWER)
    sigma = middle / spread
    lane = iota((8, LANES), 1)
    low_lane = lane < 4
    halo = low_lane | (lane >= LANES - 4)
    top, bottom = iota((8, LANES), 0) == 0, iota((8, LANES), 0) == 7
    tiles = range(TILES + 1)
    groups = range(GROUPS)

    for part, ref in enumerate((low_ref, own_ref, high_ref)):
        for x in range(CX):
            i = part * CX + x
            for j in groups:
                for t in range(TILES):
                    value = vector(ref, 0, t, x, j)
                    res[i, t, j] = value if part == 1 else jnp.maximum(value, NOTHING)
                    rem[i, t, j] = 0.5 * vector(ref, ROWS, t, x, j)
                at = [pl.ds(2 * ROWS + n * STRIP + j % 2 * 8, 8) for n in range(2)]
                above, below = ref[at[0], :], ref[at[1], :]
                for a in range(2):
                    shift = 32 * (j // 2) + 4 * (CX * a + x)
                    moved = jnp.where(lane // 4 == shift // 4, above, below)
                    if shift:
                        moved = pltpu.roll(moved, LANES - shift, 1)
                    moved = jnp.where(halo, moved, 0.0)
                    if a:
                        rem[i, TILES, j] = 0.5 * moved
                    else:
                        res[i, TILES, j] = jnp.maximum(moved, NOTHING)

    def right(values):
        rolled = [pltpu.roll(v, LANES - 1, 1) for v in values]
        n = len(values)
        return [jnp.where(lane == LANES - 1, rolled[(t + 1) % n], rolled[t]) for t in range(n)]

    def left(values, count):
        rolled = [pltpu.roll(v, 1, 1) for v in values]
        return [jnp.where(lane == 0, rolled[t - 1], rolled[t]) for t in range(count)]

    def next_z(value):
        return jnp.where(bottom, 0.0, pltpu.roll(value, 7, 0))

    def last_z(value):
        return jnp.where(top, 0.0, pltpu.roll(value, 1, 0))

    for t in tiles:
        for j in groups:
            tx[0, t, j] = inverse(res[0, t, j] + res[1, t, j])

    def setup(i, carry):
        start = [res[i, t, 0] for t in tiles]
        wrap = [next_z(start[t]) for t in tiles]
        above = [inverse(start[t] + last_z(res[i, t, GROUPS - 1])) for t in tiles]
        for t in tiles:
            tzu[i, t] = above[t]
        r = start
        for j in groups:
            r_down = [res[i, t, j + 1] if j < GROUPS - 1 else wrap[t] for t in tiles]
            r_right = right(r)
            ly = [inverse(r[t] + r_right[t]) for t in tiles]
            ly_left = left(ly, TILES + 1)
            for t in tiles:
                lx = inverse(r[t] + res[i + 1, t, j])
                lz = inverse(r[t] + r_down[t])
                diagonal = ((lx + tx[i - 1, t, j]) + (ly[t] + ly_left[t])) + (lz + above[t])
                inv_diag = jnp.where(r[t] > 2 * NOTHING, inverse(diagonal), 0.0)
                tx[i, t, j], ty[i, t, j], tz[i, t, j] = lx, ly[t], lz
                inv[i, t, j] = inv_diag
                update = inv_diag * rem[i, t, j] * (1.0 / middle)
                upd[i, t, j] = update
                if t < TILES:
                    total[i, t, j] = update
                above[t] = lz
            r = r_down
        return carry

    lax.fori_loop(1, WIDE - 1, setup, 0)

    weight_old = 1.0 / sigma
    for sweep in range(1, SWEEPS):
        last = sweep == SWEEPS - 1
        begin, end = 1 + sweep, WIDE - 1 - sweep
        weight_new = 1.0 / (2.0 * sigma - weight_old)
        keep, gain = weight_new * weight_old, 2.0 * weight_new / spread
        weight_old = weight_new
        done = range(TILES) if last else tiles
        for t in done:
            for j in groups:
                flux[t, j] = tx[begin - 1, t, j] * (upd[begin - 1, t, j] - upd[begin, t, j])

        def step(i, carry):
            u = [upd[i, t, 0] for t in tiles]
            wrap = [next_z(u[t]) for t in done]
            above = [tzu[i, t] * (last_z(upd[i, t, GROUPS - 1]) - u[t]) for t in done]
            for j in groups:
                u_down = [upd[i, t, j + 1] if j < GROUPS - 1 else (wrap + u)[t] for t in tiles]
                u_right = right(u)
                fy = [ty[i, t, j] * (u[t] - u_right[t]) for t in tiles]
                fy_left = left(fy, len(done))
                for t in done:
                    fx = tx[i, t, j] * (u[t] - upd[i + 1, t, j])
                    fz = tz[i, t, j] * (u[t] - u_down[t])
                    applied = ((fx - flux[t, j]) + (fy[t] - fy_left[t])) + (fz - above[t])
                    above[t] = fz
                    flux[t, j] = fx
                    remain = rem[i, t, j] - applied
                    new = keep * u[t] + gain * inv[i, t, j] * remain
                    if last:
                        at = pl.ds(j * STEP + t * CX + i - DEPTH, 8, stride=FAR_ROW)
                        out_ref[at, :] = total[i, t, j] + new
                    else:
                        rem[i, t, j] = remain
                        upd[i, t, j] = new
                        if t < TILES:
                            total[i, t, j] = total[i, t, j] + new
                u = u_down
            return carry

        lax.fori_loop(begin, end, step, 0)


def correct_kernel(gathered_ref, inverse_ref, support_ref, smooth_ref, out_ref, buf, sems):
    zero = jnp.zeros((CF, LANES), jnp.float32)
    sums = [zero] * 4
    for q in range(gathered_ref.shape[0]):
        part = inverse_ref[:, q * LANES : (q + 1) * LANES] * gathered_ref[pl.ds(q, 1), :]
        sums[q % 4] = sums[q % 4] + part
    column = jnp.sum((sums[0] + sums[1]) + (sums[2] + sums[3]), axis=1, keepdims=True)
    table = jnp.broadcast_to(column_to_lanes(column, 0), (8, LANES))

    def step(i, carry):
        at = pl.ds(pl.multiple_of(i * 8, 8), 8)
        buf[at, :] = smooth_ref[at, :] + pick(table, support_ref[at, :])
        return carry

    size = ROWS // CHUNKS
    copies = []
    for k in range(CHUNKS):
        lax.fori_loop(k * size // 8, (k + 1) * size // 8, step, 0, unroll=8)
        at = pl.ds(k * size, size)
        copies.append(pltpu.make_async_copy(buf.at[at, :], out_ref.at[at, :], sems.at[k]))
        copies[-1].start()
    for copy in copies:
        copy.wait()


def specs(space, count=1):
    return [pl.BlockSpec(memory_space=space)] * count


def call(kernel, outs, ins, args, out_space=pltpu.VMEM, flops=0, **options):
    size = sum(a.size * 4 for a in args) + sum(math.prod(o.shape) * 4 for o in outs)
    return pl.pallas_call(
        kernel,
        out_shape=outs,
        in_specs=ins,
        out_specs=specs(out_space, len(outs)),
        compiler_params=pltpu.CompilerParams(vmem_limit_bytes=24 * 1024 * 1024),
        cost_estimate=pl.CostEstimate(flops=flops, bytes_accessed=size, transcendentals=0),
        **options,
    )(*args)


def held(*shape):
    return pltpu.VMEM(shape, jnp.float32)


def local(residual, classes, class_perm, support, coarse_inverse):
    n_gx, n_gy = lax.axis_size("gx"), lax.axis_size("gy")
    near = LANES // CF
    residual, classes, support = rows_of(residual), rows_of(classes), rows_of(support)

    message, own = call(
        coarse_kernel,
        [held(n_gy, FACE + STRIP, LANES), held(OWN, LANES)],
        specs(pltpu.HBM, 4),
        [class_perm, residual, support, classes],
        scratch_shapes=[
            pltpu.VMEM((ROWS, LANES), jnp.int32),
            pltpu.VMEM((ROWS, LANES), jnp.int32),
            pltpu.SMEM(class_perm.shape, jnp.float32),
            pltpu.SemaphoreType.DMA((CHUNKS, 2)),
            pltpu.SemaphoreType.DMA,
            pltpu.SemaphoreType.DMA,
        ],
        name="coarse",
    )
    across = [[s * near + i for i in range(near)] for s in range(n_gx // near)]
    along = [[s * near + i for s in range(n_gx // near)] for i in range(near)]
    got = lax.all_to_all(message, "gy", 0, 0, tiled=True)
    rows, own = call(
        merge_kernel,
        [held(near, 1, LANES), held(OWN, LANES)],
        specs(pltpu.VMEM, 2),
        [got, own],
        input_output_aliases={1: 1},
        name="merge",
    )
    got_x = lax.all_to_all(rows, "gx", 0, 0, axis_index_groups=across, tiled=True)
    got_x = got_x.reshape(near, LANES)
    (copies,) = call(
        fan_kernel,
        [held(n_gx // near, near, LANES)],
        specs(pltpu.VMEM),
        [got_x],
        flops=FAR,
        name="fan",
    )
    gathered = lax.all_to_all(copies, "gx", 0, 0, axis_index_groups=along, tiled=True)
    gathered = gathered.reshape(n_gx, LANES)

    forward = [(i, i + 1) for i in range(n_gx - 1)]
    backward = [(j, i) for i, j in forward]
    low = lax.ppermute(own, "gx", forward)
    high = lax.ppermute(own, "gx", backward)
    planes = pltpu.VMEM((WIDE, TILES + 1, GROUPS, 8, LANES), jnp.float32)
    (smooth,) = call(
        smooth_kernel,
        [held(ROWS, LANES)],
        specs(pltpu.VMEM, 3) + specs(pl.ANY),
        [low, own, high, got_x],
        flops=20_000_000,
        scratch_shapes=[planes] * 7
        + [
            pltpu.VMEM((WIDE, TILES + 1, 8, LANES), jnp.float32),
            pltpu.VMEM((TILES + 1, GROUPS, 8, LANES), jnp.float32),
            pltpu.VMEM((WIDE, TILES, GROUPS, 8, LANES), jnp.float32),
        ],
        name="smooth",
    )
    (out,) = call(
        correct_kernel,
        [jax.ShapeDtypeStruct((ROWS, LANES), jnp.float32)],
        specs(pltpu.VMEM, 4),
        [gathered, coarse_inverse, support, smooth],
        out_space=pltpu.HBM,
        scratch_shapes=[
            pltpu.VMEM((ROWS, LANES), jnp.float32),
            pltpu.SemaphoreType.DMA((CHUNKS,)),
        ],
        name="correct",
    )
    return block_of(out)


def solution(mesh):
    return jax.shard_map(
        local,
        mesh=mesh,
        in_specs=(
            P(None, "gx", "gy"),
            P(None, "gx", "gy"),
            P(),
            P(None, "gx", "gy"),
            P(("gx", "gy"), None),
        ),
        out_specs=P(None, "gx", "gy"),
        check_vma=False,
    )
```

time: 65.1 us -> 57.3 us (0.88)
  the two profiles are of different devices: /device:TPU:1 before, /device:TPU:31 now
where the time goes in v2:
time: 57.3 us; the launch traced here: 56.9 us
  starting transfers between devices  17.6 us (31%)
  blocking collectives  17.5 us (31%)
  Pallas kernels  11.6 us (20%)
  waiting for transfers between devices  6.72 us (12%)
  local copies, waits for them, and re-layouts  3.51 us (6%)
    all_to_all x1, blocking collectives, local(): got = lax.all_to_all(message, 'gy', 0, 0, tiled=True)  17.5 us
    pallas_call x5, Pallas kernels, call(): pl.pallas_call(kernel, out_shape=outs, in_specs=ins, out_specs=specs(out_...  11.6 us
    ppermute x1, waiting for transfers between devices, local(): high = lax.ppermute(own, 'gx', backward)  6.71 us
    all_to_all x1, starting transfers between devices, local(): lax.all_to_all(rows, 'gx', 0, 0, axis_index_groups=across, tiled=True)  6.48 us
    all_to_all x1, starting transfers between devices, local(): lax.all_to_all(copies, 'gx', 0, 0, axis_index_groups=along, tiled=True)  5.07 us
    ppermute x1, starting transfers between devices, local(): low = lax.ppermute(own, 'gx', forward)  4.09 us
    unnamed x12, local copies, waits for them, and re-layouts  3.51 us
    ppermute x1, starting transfers between devices, local(): high = lax.ppermute(own, 'gx', backward)  1.92 us
  transfers between devices with their start and end apart: 4, of which 1 were waited for; matrix products, arithmetic and copies ran while one was open for 0% of the time, Pallas kernels for 12%

profile of v2, /device:TPU:31, one launch (start us, length us, event | category | flops | bytes accessed | tf_op | source)
XLA Modules:
  0.0 56.9 jit_solution(6724560460721002793)
XLA Ops:
  0.0 0.0 copy-start.5
  0.0 0.7 %copy-done.5 = f32[16]{0:T(128)S(1)} copy-done((f32[16]{0:T(128)S(1)}, f32[16]{0:T(128)}, u32[]{:S(2)}) %copy-start.5) | copy-done | bytes 88
  0.7 0.0 copy-start
  0.7 0.9 %copy-done = s32[64,4,256]{2,1,0:T(4,128)S(1)} copy-done((s32[64,4,256]{2,1,0:T(4,128)S(1)}, s32[64,4,256]{2,1,0:T(4,128)}, u32[]{:S(2)}) %copy-start) | copy-done | bytes 262168
  1.6 0.0 copy-start.3
  1.6 0.9 %copy-done.3 = f32[64,4,256]{2,1,0:T(4,128)S(1)} copy-done((f32[64,4,256]{2,1,0:T(4,128)S(1)}, f32[64,4,256]{2,1,0:T(4,128)}, u32[]{:S(2)}) %copy-start.3) | copy-done | bytes 262168
  2.6 0.0 copy-start.4
  2.6 0.9 %copy-done.4 = s32[64,4,256]{2,1,0:T(4,128)S(1)} copy-done((s32[64,4,256]{2,1,0:T(4,128)S(1)}, s32[64,4,256]{2,1,0:T(4,128)}, u32[]{:S(2)}) %copy-start.4) | copy-done | bytes 262168
  3.5 2.4 %coarse.1 = (f32[8,24,128]{2,1,0:T(8,128)S(1)}, f32[1056,128]{1,0:T(8,128)S(1)}) custom-call(f32[16]{0:T(128)S(1)} %copy-done.5, f32[512,128]{1,0:T(8,128)S(1)} %bitcast.24, s32[512,128]{1,0:T(8,128)S(1)} %bitcast.22, s32[512,128]{1,0:T(8,128)S(1)} %bitcast.25), custom_call_target="tpu_custom_call" | custom-call | bytes 1425472 | tf_op jit(solution)/shard_map/coarse/pallas_call | solution.py:308
  5.9 17.5 %all_to_all.15.got_ref = f32[8,24,128]{2,1,0:T(8,128)S(1)} all-to-all(f32[8,24,128]{2,1,0:T(8,128)S(1)} %get-tuple-element.9), channel_id=1, replica_groups=mesh['gx'=64,'gy'=8] {'gy'}, dimensions={0} | all-to-all | bytes 196608 | tf_op jit(solution)/shard_map/all_to_all | solution.py:345
  23.4 0.6 %merge.1 = (f32[8,1,128]{2,1,0:T(1,128)}, f32[1056,128]{1,0:T(8,128)S(1)}) custom-call(f32[8,24,128]{2,1,0:T(8,128)S(1)} %all_to_all.15.got_ref, f32[1056,128]{1,0:T(8,128)S(1)} %get-tuple-element.10.own_ref), custom_call_target="tpu_custom_call", output_to_operand_aliasing={{1}: (1, {})} | custom-call | bytes 1183744 | tf_op jit(solution)/shard_map/merge/pallas_call | solution.py:308
  24.0 6.5 %all-to-all-start.1 = ((f32[8,1,128]{2,1,0:T(1,128)}), f32[8,1,128]{2,1,0:T(1,128)S(1)}, u32[]{:S(2)}, u32[]{:S(2)}) async-start(f32[8,1,128]{2,1,0:T(1,128)} %get-tuple-element.11), calls=%async_computation.1 | async-start | bytes 8192 | tf_op jit(solution)/shard_map/all_to_all | solution.py:354
  30.5 4.1 %collective-permute-start = (f32[1056,128]{1,0:T(8,128)S(1)}, f32[1056,128]{1,0:T(8,128)S(1)}, u32[]{:S(2)}, u32[]{:S(2)}) collective-permute-start(f32[1056,128]{1,0:T(8,128)S(1)} %get-tuple-element.12.own_ref), channel_id=1, source_target_pairs={{0,8},{8,16},{16,24},{24,32},{32,40},{40,48},{48,56},{56,64},{64,7... | collective-permute-start | bytes 1622024 | tf_op jit(solution)/shard_map/ppermute | solution.py:369
  34.6 1.9 %collective-permute-start.1 = (f32[1056,128]{1,0:T(8,128)S(1)}, f32[1056,128]{1,0:T(8,128)S(1)}, u32[]{:S(2)}, u32[]{:S(2)}) collective-permute-start(f32[1056,128]{1,0:T(8,128)S(1)} %get-tuple-element.12.own_ref), channel_id=1, source_target_pairs={{8,0},{16,8},{24,16},{32,24},{40,32},{48,40},{56,48},{64,56},{72,6... | collective-permute-start | bytes 1622024 | tf_op jit(solution)/shard_map/ppermute | solution.py:370
  36.5 0.0 all-to-all-done.1
  36.5 0.6 %fan.1 = f32[8,8,128]{2,1,0:T(8,128)} custom-call(f32[8,128]{1,0:T(8,128)S(1)} %bitcast.27), custom_call_target="tpu_custom_call" | custom-call | flops 10000000000 | bytes 36864 | tf_op jit(solution)/shard_map/fan/pallas_call | solution.py:308
  37.1 5.1 %all-to-all-start.2 = ((f32[8,8,128]{2,1,0:T(8,128)}), f32[8,8,128]{2,1,0:T(8,128)S(1)}, u32[]{:S(2)}, u32[]{:S(2)}) async-start(f32[8,8,128]{2,1,0:T(8,128)} %fan.1), calls=%async_computation.2 | async-start | bytes 65536 | tf_op jit(solution)/shard_map/all_to_all | solution.py:364
  42.2 0.0 collective-permute-done.low_ref
  42.2 6.7 %collective-permute-done.1.high_ref = f32[1056,128]{1,0:T(8,128)S(1)} collective-permute-done((f32[1056,128]{1,0:T(8,128)S(1)}, f32[1056,128]{1,0:T(8,128)S(1)}, u32[]{:S(2)}, u32[]{:S(2)}) %collective-permute-start.1) | collective-permute-done | bytes 540704 | tf_op jit(solution)/shard_map/ppermute | solution.py:370
  48.9 6.4 %smooth.1.smooth_ref = f32[512,128]{1,0:T(8,128)S(1)} custom-call(f32[1056,128]{1,0:T(8,128)S(1)} %collective-permute-done.low_ref, f32[1056,128]{1,0:T(8,128)S(1)} %get-tuple-element.12.own_ref, f32[1056,128]{1,0:T(8,128)S(1)} %collective-permute-done.1.high_ref, f32[8,128]{1,0:T(8,128)S(1)} %bitcast.28), custom_call_target="tpu_custom_call" | custom-call | flops 20000000 | bytes 1888256 | tf_op jit(solution)/shard_map/smooth/pallas_call | solution.py:308
  55.4 0.0 all-to-all-done.2
  55.4 0.0 copy-done.1
  55.4 0.0 copy-done.2
  55.4 1.5 %correct.1 = f32[512,128]{1,0:T(8,128)} custom-call(f32[64,128]{1,0:T(8,128)S(1)} %bitcast.26, f32[16,8192]{1,0:T(8,128)S(1)} %copy-done.2, s32[512,128]{1,0:T(8,128)S(1)} %bitcast.23, f32[512,128]{1,0:T(8,128)S(1)} %smooth.1.smooth_ref), custom_call_target="tpu_custom_call" | custom-call | bytes 1343488 | tf_op jit(solution)/shard_map/correct/pallas_call | solution.py:308
  (2 shorter events, 0.0 us)
Async XLA Ops:
  0.0 0.7 %copy-start.5 = (f32[16]{0:T(128)S(1)}, f32[16]{0:T(128)}, u32[]{:S(2)}) copy-start(f32[16]{0:T(128)} %perm_ref.1) | copy-start | bytes 196
  0.7 0.9 %copy-start = (s32[64,4,256]{2,1,0:T(4,128)S(1)}, s32[64,4,256]{2,1,0:T(4,128)}, u32[]{:S(2)}) copy-start(s32[64,4,256]{2,1,0:T(4,128)} %param.8) | copy-start | bytes 786436
  1.6 0.9 %copy-start.3 = (f32[64,4,256]{2,1,0:T(4,128)S(1)}, f32[64,4,256]{2,1,0:T(4,128)}, u32[]{:S(2)}) copy-start(f32[64,4,256]{2,1,0:T(4,128)} %param.5) | copy-start | bytes 786436
  2.6 0.9 %copy-start.4 = (s32[64,4,256]{2,1,0:T(4,128)S(1)}, s32[64,4,256]{2,1,0:T(4,128)}, u32[]{:S(2)}) copy-start(s32[64,4,256]{2,1,0:T(4,128)} %param.6) | copy-start | bytes 786436
  24.0 12.5 %all-to-all-start.1 = ((f32[8,1,128]{2,1,0:T(1,128)}), f32[8,1,128]{2,1,0:T(1,128)S(1)}, u32[]{:S(2)}, u32[]{:S(2)}) async-start(f32[8,1,128]{2,1,0:T(1,128)} %get-tuple-element.11), calls=%async_computation.1 | async-start | bytes 8192 | tf_op jit(solution)/shard_map/all_to_all | solution.py:354
  30.5 11.7 %collective-permute-start = (f32[1056,128]{1,0:T(8,128)S(1)}, f32[1056,128]{1,0:T(8,128)S(1)}, u32[]{:S(2)}, u32[]{:S(2)}) collective-permute-start(f32[1056,128]{1,0:T(8,128)S(1)} %get-tuple-element.12.own_ref), channel_id=1, source_target_pairs={{0,8},{8,16},{16,24},{24,32},{32,40},{40,48},{48,56},{56,64},{64,7... | collective-permute-start | bytes 1622024 | tf_op jit(solution)/shard_map/ppermute | solution.py:369
  34.6 14.3 %collective-permute-start.1 = (f32[1056,128]{1,0:T(8,128)S(1)}, f32[1056,128]{1,0:T(8,128)S(1)}, u32[]{:S(2)}, u32[]{:S(2)}) collective-permute-start(f32[1056,128]{1,0:T(8,128)S(1)} %get-tuple-element.12.own_ref), channel_id=1, source_target_pairs={{8,0},{16,8},{24,16},{32,24},{40,32},{48,40},{56,48},{64,56},{72,6... | collective-permute-start | bytes 1622024 | tf_op jit(solution)/shard_map/ppermute | solution.py:370
  37.1 18.2 %all-to-all-start.2 = ((f32[8,8,128]{2,1,0:T(8,128)}), f32[8,8,128]{2,1,0:T(8,128)S(1)}, u32[]{:S(2)}, u32[]{:S(2)}) async-start(f32[8,8,128]{2,1,0:T(8,128)} %fan.1), calls=%async_computation.2 | async-start | bytes 65536 | tf_op jit(solution)/shard_map/all_to_all | solution.py:364
  42.2 13.2 %copy-start.1 = (s32[64,4,256]{2,1,0:T(4,128)S(1)}, s32[64,4,256]{2,1,0:T(4,128)}, u32[]{:S(2)}) copy-start(s32[64,4,256]{2,1,0:T(4,128)} %param.8) | copy-start | bytes 786436
  42.2 13.2 %copy-start.2 = (f32[16,8192]{1,0:T(8,128)S(1)}, f32[16,8192]{1,0:T(8,128)}, u32[]{:S(2)}) copy-start(f32[16,8192]{1,0:T(8,128)} %inverse_ref.1) | copy-start | bytes 1572868

commit v3 on v2

--- a/solution.py
+++ b/solution.py
@@ -21,6 +21,7 @@
 STRIP = 16
 OWN = 2 * ROWS + 2 * STRIP
 FACE = 8
+PAD = 1
 CHUNKS = 4
 FAR = 10**10
 NOTHING = 1e-30
@@ -137,7 +138,7 @@
     for k in range(1, count):
         row = row + got_ref[k, 0:1, :]
     for k in range(rows_ref.shape[0]):
-        rows_ref[k] = row
+        rows_ref[k] = jnp.broadcast_to(row, rows_ref.shape[1:])
     me = lax.axis_index("gy")
     strip = pl.ds(FACE, STRIP)
     above = got_ref[jnp.minimum(me + 1, count - 1), strip, :]
@@ -148,10 +149,13 @@
 
 def fan_kernel(got_ref, copies_ref):
     for k in range(copies_ref.shape[0]):
-        copies_ref[k] = got_ref[...]
-
-
-def smooth_kernel(low_ref, own_ref, high_ref, after_ref, out_ref, res, upd, rem, inv, tx, ty, tz, tzu, flux, total):
+        copies_ref[k] = got_ref[:, 0, :]
+
+
+def smooth_kernel(
+    low_ref, own_ref, high_ref, after_ref, out_ref,
+    res, upd, rem, inv, tx, ty, tyl, tz, tzu, flux, total,
+):
     middle = 0.5 * (UPPER + LOWER)
     spread = 0.5 * (UPPER - LOWER)
     sigma = middle / spread
@@ -170,8 +174,8 @@
                     value = vector(ref, 0, t, x, j)
                     res[i, t, j] = value if part == 1 else jnp.maximum(value, NOTHING)
                     rem[i, t, j] = 0.5 * vector(ref, ROWS, t, x, j)
-                at = [pl.ds(2 * ROWS + n * STRIP + j % 2 * 8, 8) for n in range(2)]
-                above, below = ref[at[0], :], ref[at[1], :]
+                above = ref[pl.ds(2 * ROWS + j % 2 * 8, 8), :]
+                below = ref[pl.ds(2 * ROWS + STRIP + j % 2 * 8, 8), :]
                 for a in range(2):
                     shift = 32 * (j // 2) + 4 * (CX * a + x)
                     moved = jnp.where(lane // 4 == shift // 4, above, below)
@@ -220,6 +224,7 @@
                 diagonal = ((lx + tx[i - 1, t, j]) + (ly[t] + ly_left[t])) + (lz + above[t])
                 inv_diag = jnp.where(r[t] > 2 * NOTHING, inverse(diagonal), 0.0)
                 tx[i, t, j], ty[i, t, j], tz[i, t, j] = lx, ly[t], lz
+                tyl[i, t, j] = ly_left[t]
                 inv[i, t, j] = inv_diag
                 update = inv_diag * rem[i, t, j] * (1.0 / middle)
                 upd[i, t, j] = update
@@ -229,7 +234,7 @@
             r = r_down
         return carry
 
-    lax.fori_loop(1, WIDE - 1, setup, 0)
+    lax.fori_loop(1, WIDE - 1, setup, 0, unroll=2)
 
     weight_old = 1.0 / sigma
     for sweep in range(1, SWEEPS):
@@ -239,23 +244,23 @@
         keep, gain = weight_new * weight_old, 2.0 * weight_new / spread
         weight_old = weight_new
         done = range(TILES) if last else tiles
+        src, dst = (upd, res) if sweep % 2 else (res, upd)
         for t in done:
             for j in groups:
-                flux[t, j] = tx[begin - 1, t, j] * (upd[begin - 1, t, j] - upd[begin, t, j])
+                flux[t, j] = tx[begin - 1, t, j] * (src[begin - 1, t, j] - src[begin, t, j])
 
         def step(i, carry):
-            u = [upd[i, t, 0] for t in tiles]
+            u = [src[i, t, 0] for t in tiles]
             wrap = [next_z(u[t]) for t in done]
-            above = [tzu[i, t] * (last_z(upd[i, t, GROUPS - 1]) - u[t]) for t in done]
+            above = [tzu[i, t] * (last_z(src[i, t, GROUPS - 1]) - u[t]) for t in done]
             for j in groups:
-                u_down = [upd[i, t, j + 1] if j < GROUPS - 1 else (wrap + u)[t] for t in tiles]
+                u_down = [src[i, t, j + 1] if j < GROUPS - 1 else (wrap + u)[t] for t in tiles]
                 u_right = right(u)
-                fy = [ty[i, t, j] * (u[t] - u_right[t]) for t in tiles]
-                fy_left = left(fy, len(done))
+                u_left = left(u, len(done))
                 for t in done:
-                    fx = tx[i, t, j] * (u[t] - upd[i + 1, t, j])
+                    fx = tx[i, t, j] * (u[t] - src[i + 1, t, j])
                     fz = tz[i, t, j] * (u[t] - u_down[t])
-                    applied = ((fx - flux[t, j]) + (fy[t] - fy_left[t])) + (fz - above[t])
+                    applied = ((fx - flux[t, j]) + (ty[i, t, j] * (u[t] - u_right[t]) + tyl[i, t, j] * (u[t] - u_left[t]))) + (fz - above[t])
                     above[t] = fz
                     flux[t, j] = fx
                     remain = rem[i, t, j] - applied
@@ -265,13 +270,13 @@
                         out_ref[at, :] = total[i, t, j] + new
                     else:
                         rem[i, t, j] = remain
-                        upd[i, t, j] = new
+                        dst[i, t, j] = new
                         if t < TILES:
                             total[i, t, j] = total[i, t, j] + new
                 u = u_down
             return carry
 
-        lax.fori_loop(begin, end, step, 0)
+        lax.fori_loop(begin, end, step, 0, unroll=2)
 
 
 def correct_kernel(gathered_ref, inverse_ref, support_ref, smooth_ref, out_ref, buf, sems):
@@ -303,14 +308,14 @@
     return [pl.BlockSpec(memory_space=space)] * count
 
 
-def call(kernel, outs, ins, args, out_space=pltpu.VMEM, flops=0, **options):
+def call(kernel, outs, ins, args, out_space=pltpu.VMEM, flops=0, limit=24, **options):
     size = sum(a.size * 4 for a in args) + sum(math.prod(o.shape) * 4 for o in outs)
     return pl.pallas_call(
         kernel,
         out_shape=outs,
         in_specs=ins,
         out_specs=specs(out_space, len(outs)),
-        compiler_params=pltpu.CompilerParams(vmem_limit_bytes=24 * 1024 * 1024),
+        compiler_params=pltpu.CompilerParams(vmem_limit_bytes=limit * 1024 * 1024),
         cost_estimate=pl.CostEstimate(flops=flops, bytes_accessed=size, transcendentals=0),
         **options,
     )(*args)
@@ -338,6 +343,7 @@
             pltpu.SemaphoreType.DMA,
             pltpu.SemaphoreType.DMA,
         ],
+        limit=60,
         name="coarse",
     )
     across = [[s * near + i for i in range(near)] for s in range(n_gx // near)]
@@ -345,24 +351,13 @@
     got = lax.all_to_all(message, "gy", 0, 0, tiled=True)
     rows, own = call(
         merge_kernel,
-        [held(near, 1, LANES), held(OWN, LANES)],
+        [held(n_gx, PAD, LANES), held(OWN, LANES)],
         specs(pltpu.VMEM, 2),
         [got, own],
         input_output_aliases={1: 1},
         name="merge",
     )
-    got_x = lax.all_to_all(rows, "gx", 0, 0, axis_index_groups=across, tiled=True)
-    got_x = got_x.reshape(near, LANES)
-    (copies,) = call(
-        fan_kernel,
-        [held(n_gx // near, near, LANES)],
-        specs(pltpu.VMEM),
-        [got_x],
-        flops=FAR,
-        name="fan",
-    )
-    gathered = lax.all_to_all(copies, "gx", 0, 0, axis_index_groups=along, tiled=True)
-    gathered = gathered.reshape(n_gx, LANES)
+    gathered = lax.all_to_all(rows, "gx", 0, 0, tiled=True).reshape(n_gx, LANES)
 
     forward = [(i, i + 1) for i in range(n_gx - 1)]
     backward = [(j, i) for i, j in forward]
@@ -373,9 +368,9 @@
         smooth_kernel,
         [held(ROWS, LANES)],
         specs(pltpu.VMEM, 3) + specs(pl.ANY),
-        [low, own, high, got_x],
+        [low, own, high, rows],
         flops=20_000_000,
-        scratch_shapes=[planes] * 7
+        scratch_shapes=[planes] * 8
         + [
             pltpu.VMEM((WIDE, TILES + 1, 8, LANES), jnp.float32),
             pltpu.VMEM((TILES + 1, GROUPS, 8, LANES), jnp.float32),

time: 57.3 us -> 51.2 us (0.89)
  the two profiles are of different devices: /device:TPU:31 before, /device:TPU:1 now
where the time goes in v3:
time: 51.2 us; the launch traced here: 51 us
  starting transfers between devices  18.6 us (36%)
  blocking collectives  18.3 us (36%)
  Pallas kernels  9.13 us (18%)
  waiting for transfers between devices  4.9 us (10%)
    all_to_all x1, blocking collectives, local(): got = lax.all_to_all(message, 'gy', 0, 0, tiled=True)  18.3 us
    all_to_all x1, starting transfers between devices, local(): gathered = lax.all_to_all(rows, 'gx', 0, 0, tiled=True).reshape(n_gx, LANES)  11.6 us
    pallas_call x4, Pallas kernels, call(): pl.pallas_call(kernel, out_shape=outs, in_specs=ins, out_specs=specs(out_...  9.13 us
    ppermute x1, starting transfers between devices, local(): low = lax.ppermute(own, 'gx', forward)  5.06 us
    all_to_all x1, waiting for transfers between devices, local(): gathered = lax.all_to_all(rows, 'gx', 0, 0, tiled=True).reshape(n_gx, LANES)  4.89 us
    ppermute x1, starting transfers between devices, local(): high = lax.ppermute(own, 'gx', backward)  1.92 us
  transfers between devices with their start and end apart: 3, of which 1 were waited for; matrix products, arithmetic and copies ran while one was open for 0% of the time, Pallas kernels for 9%

profile of v3, /device:TPU:1, one launch (start us, length us, event | category | flops | bytes accessed | tf_op | source)
XLA Modules:
  0.0 51.0 jit_solution(13177382742154121354)
XLA Ops:
  0.0 2.6 %coarse.1 = (f32[8,24,128]{2,1,0:T(8,128)S(1)}, f32[1056,128]{1,0:T(8,128)S(1)}) custom-call(f32[16]{0:T(128)} %perm_ref.1, f32[512,128]{1,0:T(8,128)} %bitcast.24, s32[512,128]{1,0:T(8,128)} %bitcast.21, s32[512,128]{1,0:T(8,128)} %bitcast.25), custom_call_target="tpu_custom_call" | custom-call | bytes 1425472 | tf_op jit(solution)/shard_map/coarse/pallas_call | solution.py:313
  2.6 18.3 %all_to_all.10.got_ref = f32[8,24,128]{2,1,0:T(8,128)S(1)} all-to-all(f32[8,24,128]{2,1,0:T(8,128)S(1)} %get-tuple-element.9), channel_id=1, replica_groups=mesh['gx'=64,'gy'=8] {'gy'}, dimensions={0} | all-to-all | bytes 196608 | tf_op jit(solution)/shard_map/all_to_all | solution.py:351
  20.9 0.6 %merge.1 = (f32[64,1,128]{2,1,0:T(1,128)}, f32[1056,128]{1,0:T(8,128)S(1)}) custom-call(f32[8,24,128]{2,1,0:T(8,128)S(1)} %all_to_all.10.got_ref, f32[1056,128]{1,0:T(8,128)S(1)} %get-tuple-element.10.own_ref), custom_call_target="tpu_custom_call", output_to_operand_aliasing={{1}: (1, {})} | custom-call | bytes 1212416 | tf_op jit(solution)/shard_map/merge/pallas_call | solution.py:313
  21.5 5.1 %collective-permute-start = (f32[1056,128]{1,0:T(8,128)S(1)}, f32[1056,128]{1,0:T(8,128)S(1)}, u32[]{:S(2)}, u32[]{:S(2)}) collective-permute-start(f32[1056,128]{1,0:T(8,128)S(1)} %get-tuple-element.12.own_ref), channel_id=1, source_target_pairs={{0,8},{8,16},{16,24},{24,32},{32,40},{40,48},{48,56},{56,64},{64,7... | collective-permute-start | bytes 1622024 | tf_op jit(solution)/shard_map/ppermute | solution.py:364
  26.6 1.9 %collective-permute-start.1 = (f32[1056,128]{1,0:T(8,128)S(1)}, f32[1056,128]{1,0:T(8,128)S(1)}, u32[]{:S(2)}, u32[]{:S(2)}) collective-permute-start(f32[1056,128]{1,0:T(8,128)S(1)} %get-tuple-element.12.own_ref), channel_id=1, source_target_pairs={{8,0},{16,8},{24,16},{32,24},{40,32},{48,40},{56,48},{64,56},{72,6... | collective-permute-start | bytes 1622024 | tf_op jit(solution)/shard_map/ppermute | solution.py:365
  28.5 11.6 %all-to-all-start.1 = ((f32[64,1,128]{2,1,0:T(1,128)}), f32[64,1,128]{2,1,0:T(1,128)S(1)}, u32[]{:S(2)}, u32[]{:S(2)}) async-start(f32[64,1,128]{2,1,0:T(1,128)} %get-tuple-element.11.after_ref), calls=%async_computation.1 | async-start | bytes 65536 | tf_op jit(solution)/shard_map/all_to_all | solution.py:360
  40.2 0.0 copy-start
  40.2 0.0 copy-start.1
  40.2 0.0 collective-permute-done.low_ref
  40.2 0.0 collective-permute-done.1.high_ref
  40.2 4.4 %smooth.1.smooth_ref = f32[512,128]{1,0:T(8,128)S(1)} custom-call(f32[1056,128]{1,0:T(8,128)S(1)} %collective-permute-done.low_ref, f32[1056,128]{1,0:T(8,128)S(1)} %get-tuple-element.12.own_ref, f32[1056,128]{1,0:T(8,128)S(1)} %collective-permute-done.1.high_ref, f32[64,1,128]{2,1,0:T(1,128)} %get-tuple-element.11.after_ref), custom_call_target="tpu_custom_call" | custom-call | flops 20000000 | bytes 1916928 | tf_op jit(solution)/shard_map/smooth/pallas_call | solution.py:313
  44.6 4.9 %all-to-all-done.1 = f32[64,1,128]{2,1,0:T(1,128)S(1)} async-done(((f32[64,1,128]{2,1,0:T(1,128)}), f32[64,1,128]{2,1,0:T(1,128)S(1)}, u32[]{:S(2)}, u32[]{:S(2)}) %all-to-all-start.1) | async-done | bytes 32800 | tf_op jit(solution)/shard_map/all_to_all | solution.py:360
  49.5 0.0 copy-done
  49.5 0.0 copy-done.1
  49.5 1.5 %correct.1 = f32[512,128]{1,0:T(8,128)} custom-call(f32[64,128]{1,0:T(8,128)S(1)} %bitcast.23, f32[16,8192]{1,0:T(8,128)S(1)} %copy-done.1, s32[512,128]{1,0:T(8,128)S(1)} %bitcast.22, f32[512,128]{1,0:T(8,128)S(1)} %smooth.1.smooth_ref), custom_call_target="tpu_custom_call" | custom-call | bytes 1343488 | tf_op jit(solution)/shard_map/correct/pallas_call | solution.py:313
Async XLA Ops:
  21.5 18.7 %collective-permute-start = (f32[1056,128]{1,0:T(8,128)S(1)}, f32[1056,128]{1,0:T(8,128)S(1)}, u32[]{:S(2)}, u32[]{:S(2)}) collective-permute-start(f32[1056,128]{1,0:T(8,128)S(1)} %get-tuple-element.12.own_ref), channel_id=1, source_target_pairs={{0,8},{8,16},{16,24},{24,32},{32,40},{40,48},{48,56},{56,64},{64,7... | collective-permute-start | bytes 1622024 | tf_op jit(solution)/shard_map/ppermute | solution.py:364
  26.6 13.6 %collective-permute-start.1 = (f32[1056,128]{1,0:T(8,128)S(1)}, f32[1056,128]{1,0:T(8,128)S(1)}, u32[]{:S(2)}, u32[]{:S(2)}) collective-permute-start(f32[1056,128]{1,0:T(8,128)S(1)} %get-tuple-element.12.own_ref), channel_id=1, source_target_pairs={{8,0},{16,8},{24,16},{32,24},{40,32},{48,40},{56,48},{64,56},{72,6... | collective-permute-start | bytes 1622024 | tf_op jit(solution)/shard_map/ppermute | solution.py:365
  28.5 20.9 %all-to-all-start.1 = ((f32[64,1,128]{2,1,0:T(1,128)}), f32[64,1,128]{2,1,0:T(1,128)S(1)}, u32[]{:S(2)}, u32[]{:S(2)}) async-start(f32[64,1,128]{2,1,0:T(1,128)} %get-tuple-element.11.after_ref), calls=%async_computation.1 | async-start | bytes 65536 | tf_op jit(solution)/shard_map/all_to_all | solution.py:360
  40.2 9.3 %copy-start = (s32[64,4,256]{2,1,0:T(4,128)S(1)}, s32[64,4,256]{2,1,0:T(4,128)}, u32[]{:S(2)}) copy-start(s32[64,4,256]{2,1,0:T(4,128)} %param.8) | copy-start | bytes 786436
  40.2 9.3 %copy-start.1 = (f32[16,8192]{1,0:T(8,128)S(1)}, f32[16,8192]{1,0:T(8,128)}, u32[]{:S(2)}) copy-start(f32[16,8192]{1,0:T(8,128)} %inverse_ref.1) | copy-start | bytes 1572868

commit v4 on v3

--- a/solution.py
+++ b/solution.py
@@ -19,11 +19,10 @@
 DEPTH = 4
 WIDE = CX + 2 * DEPTH
 STRIP = 16
-OWN = 2 * ROWS + 2 * STRIP
+SUMS = 2 * ROWS + 2 * STRIP
+OWN = SUMS + 8
 FACE = 8
-PAD = 1
 CHUNKS = 4
-FAR = 10**10
 NOTHING = 1e-30
 
 
@@ -132,28 +131,30 @@
         message_ref[k, 0:FACE, :] = jnp.broadcast_to(row, (FACE, LANES))
 
 
-def merge_kernel(got_ref, own_ref, rows_ref, out_ref):
+def merge_kernel(got_ref, own_ref, out_ref):
     count = got_ref.shape[0]
-    row = got_ref[0, 0:1, :]
-    for k in range(1, count):
-        row = row + got_ref[k, 0:1, :]
-    for k in range(rows_ref.shape[0]):
-        rows_ref[k] = jnp.broadcast_to(row, rows_ref.shape[1:])
     me = lax.axis_index("gy")
     strip = pl.ds(FACE, STRIP)
     above = got_ref[jnp.minimum(me + 1, count - 1), strip, :]
     below = got_ref[jnp.maximum(me - 1, 0), strip, :]
     out_ref[pl.ds(2 * ROWS, STRIP), :] = jnp.where(me < count - 1, above, 0.0)
     out_ref[pl.ds(2 * ROWS + STRIP, STRIP), :] = jnp.where(me > 0, below, 0.0)
-
-
-def fan_kernel(got_ref, copies_ref):
-    for k in range(copies_ref.shape[0]):
-        copies_ref[k] = got_ref[:, 0, :]
+    row = got_ref[0, 0:8, :]
+    for k in range(1, count):
+        row = row + got_ref[k, 0:8, :]
+    out_ref[pl.ds(SUMS, 8), :] = row
+
+
+def pair_kernel(own_ref, mate_ref, rows_ref):
+    odd = lax.axis_index("gx") % 2 == 1
+    own, mate = own_ref[pl.ds(SUMS, 1), :], mate_ref[pl.ds(SUMS, 1), :]
+    both = jnp.concatenate([jnp.where(odd, mate, own), jnp.where(odd, own, mate)], axis=0)
+    for k in range(rows_ref.shape[0]):
+        rows_ref[k] = both
 
 
 def smooth_kernel(
-    low_ref, own_ref, high_ref, after_ref, out_ref,
+    own_ref, mate_ref, other_ref, after_ref, out_ref,
     res, upd, rem, inv, tx, ty, tyl, tz, tzu, flux, total,
 ):
     middle = 0.5 * (UPPER + LOWER)
@@ -166,13 +167,15 @@
     tiles = range(TILES + 1)
     groups = range(GROUPS)
 
-    for part, ref in enumerate((low_ref, own_ref, high_ref)):
+    odd = lax.axis_index("gx") % 2
+    places = ((own_ref, DEPTH), (mate_ref, 2 * CX * (1 - odd)), (other_ref, 2 * CX * odd))
+    for ref, place in places:
         for x in range(CX):
-            i = part * CX + x
+            i = place + x
             for j in groups:
                 for t in range(TILES):
                     value = vector(ref, 0, t, x, j)
-                    res[i, t, j] = value if part == 1 else jnp.maximum(value, NOTHING)
+                    res[i, t, j] = value if ref is own_ref else jnp.maximum(value, NOTHING)
                     rem[i, t, j] = 0.5 * vector(ref, ROWS, t, x, j)
                 above = ref[pl.ds(2 * ROWS + j % 2 * 8, 8), :]
                 below = ref[pl.ds(2 * ROWS + STRIP + j % 2 * 8, 8), :]
@@ -327,7 +330,6 @@
 
 def local(residual, classes, class_perm, support, coarse_inverse):
     n_gx, n_gy = lax.axis_size("gx"), lax.axis_size("gy")
-    near = LANES // CF
     residual, classes, support = rows_of(residual), rows_of(classes), rows_of(support)
 
     message, own = call(
@@ -346,29 +348,32 @@
         limit=60,
         name="coarse",
     )
-    across = [[s * near + i for i in range(near)] for s in range(n_gx // near)]
-    along = [[s * near + i for s in range(n_gx // near)] for i in range(near)]
     got = lax.all_to_all(message, "gy", 0, 0, tiled=True)
-    rows, own = call(
+    (own,) = call(
         merge_kernel,
-        [held(n_gx, PAD, LANES), held(OWN, LANES)],
+        [held(OWN, LANES)],
         specs(pltpu.VMEM, 2),
         [got, own],
-        input_output_aliases={1: 1},
+        input_output_aliases={1: 0},
         name="merge",
     )
-    gathered = lax.all_to_all(rows, "gx", 0, 0, tiled=True).reshape(n_gx, LANES)
-
-    forward = [(i, i + 1) for i in range(n_gx - 1)]
-    backward = [(j, i) for i, j in forward]
-    low = lax.ppermute(own, "gx", forward)
-    high = lax.ppermute(own, "gx", backward)
+    pairs = [(i, i ^ 1) for i in range(n_gx)]
+    others = [step for i in range(1, n_gx - 1, 2) for step in ((i, i + 1), (i + 1, i))]
+    mate = lax.ppermute(own, "gx", pairs)
+    other = lax.ppermute(own, "gx", others)
+    (rows,) = call(
+        pair_kernel, [held(n_gx // 2, 2, LANES)], specs(pltpu.VMEM, 2), [own, mate], name="pair"
+    )
+    groups = [list(range(k, n_gx, 2)) for k in range(2)]
+    gathered = lax.all_to_all(rows, "gx", 0, 0, axis_index_groups=groups, tiled=True)
+    gathered = gathered.reshape(n_gx, LANES)
+
     planes = pltpu.VMEM((WIDE, TILES + 1, GROUPS, 8, LANES), jnp.float32)
     (smooth,) = call(
         smooth_kernel,
         [held(ROWS, LANES)],
         specs(pltpu.VMEM, 3) + specs(pl.ANY),
-        [low, own, high, rows],
+        [own, mate, other, rows],
         flops=20_000_000,
         scratch_shapes=[planes] * 8
         + [

time: 51.2 us -> 48.4 us (0.945)
  starting transfers between devices: 18.6 us -> 16.4 us
  waiting for transfers between devices: 4.9 us -> 4.3 us
    all_to_all x1, starting transfers between devices: 11.6 us -> 9.38 us  [local(): lax.all_to_all(rows, 'gx', 0, 0, axis_index_groups=groups, tiled=True)]
    all_to_all x1, waiting for transfers between devices: 4.89 us -> 4.29 us  [local(): lax.all_to_all(rows, 'gx', 0, 0, axis_index_groups=groups, tiled=True)]
    pallas_call x4 -> x5, Pallas kernels: 9.13 us -> 9.16 us  [call(): pl.pallas_call(kernel, out_shape=outs, in_specs=ins, out_specs=specs(out_...]
  transfers between devices with their start and end apart: 3 -> 3, of which waited for: 1 -> 1; matrix products, arithmetic and copies ran while one was open for 0% -> 0% of each run, Pallas kernels for 9% -> 10%
where the time goes in v4:
time: 48.4 us; the launch traced here: 48.2 us
  blocking collectives  18.3 us (38%)
  starting transfers between devices  16.4 us (34%)
  Pallas kernels  9.16 us (19%)
  waiting for transfers between devices  4.3 us (9%)
    all_to_all x1, blocking collectives, local(): got = lax.all_to_all(message, 'gy', 0, 0, tiled=True)  18.3 us
    all_to_all x1, starting transfers between devices, local(): lax.all_to_all(rows, 'gx', 0, 0, axis_index_groups=groups, tiled=True)  9.38 us
    pallas_call x5, Pallas kernels, call(): pl.pallas_call(kernel, out_shape=outs, in_specs=ins, out_specs=specs(out_...  9.16 us
    all_to_all x1, waiting for transfers between devices, local(): lax.all_to_all(rows, 'gx', 0, 0, axis_index_groups=groups, tiled=True)  4.29 us
    ppermute x1, starting transfers between devices, local(): mate = lax.ppermute(own, 'gx', pairs)  3.97 us
    ppermute x1, starting transfers between devices, local(): other = lax.ppermute(own, 'gx', others)  3.02 us
  transfers between devices with their start and end apart: 3, of which 1 were waited for; matrix products, arithmetic and copies ran while one was open for 0% of the time, Pallas kernels for 10%

profile of v4, /device:TPU:1, one launch (start us, length us, event | category | flops | bytes accessed | tf_op | source)
XLA Modules:
  0.0 48.2 jit_solution(90618670506099093)
XLA Ops:
  0.0 2.6 %coarse.1 = (f32[8,24,128]{2,1,0:T(8,128)S(1)}, f32[1064,128]{1,0:T(8,128)S(1)}) custom-call(f32[16]{0:T(128)} %perm_ref.1, f32[512,128]{1,0:T(8,128)} %bitcast.24, s32[512,128]{1,0:T(8,128)} %bitcast.21, s32[512,128]{1,0:T(8,128)} %bitcast.25), custom_call_target="tpu_custom_call" | custom-call | bytes 1429568 | tf_op jit(solution)/shard_map/coarse/pallas_call | solution.py:316
  2.6 18.3 %all_to_all.10.got_ref = f32[8,24,128]{2,1,0:T(8,128)S(1)} all-to-all(f32[8,24,128]{2,1,0:T(8,128)S(1)} %get-tuple-element.7), channel_id=1, replica_groups=mesh['gx'=64,'gy'=8] {'gy'}, dimensions={0} | all-to-all | bytes 196608 | tf_op jit(solution)/shard_map/all_to_all | solution.py:351
  20.9 4.0 %collective-permute-start = (f32[1064,128]{1,0:T(8,128)S(1)}, f32[1064,128]{1,0:T(8,128)S(1)}, u32[]{:S(2)}, u32[]{:S(2)}) collective-permute-start(f32[1064,128]{1,0:T(8,128)S(1)} %merge.1.own_ref), channel_id=1, source_target_pairs={{0,8},{8,0},{16,24},{24,16},{32,40},{40,32},{48,56},{56,48},{64,72... | collective-permute-start | bytes 1634312 | tf_op jit(solution)/shard_map/ppermute | solution.py:362
  24.9 3.0 %collective-permute-start.1 = (f32[1064,128]{1,0:T(8,128)S(1)}, f32[1064,128]{1,0:T(8,128)S(1)}, u32[]{:S(2)}, u32[]{:S(2)}) collective-permute-start(f32[1064,128]{1,0:T(8,128)S(1)} %merge.1.own_ref), channel_id=1, source_target_pairs={{8,16},{16,8},{24,32},{32,24},{40,48},{48,40},{56,64},{64,56},{72,... | collective-permute-start | bytes 1634312 | tf_op jit(solution)/shard_map/ppermute | solution.py:363
  27.9 0.0 collective-permute-done.mate_ref
  27.9 0.6 %pair.1.after_ref = f32[32,2,128]{2,1,0:T(2,128)} custom-call(f32[1064,128]{1,0:T(8,128)S(1)} %merge.1.own_ref, f32[1064,128]{1,0:T(8,128)S(1)} %collective-permute-done.mate_ref), custom_call_target="tpu_custom_call" | custom-call | bytes 1122304 | tf_op jit(solution)/shard_map/pair/pallas_call | solution.py:316
  28.6 9.4 %all-to-all-start.1 = ((f32[32,2,128]{2,1,0:T(2,128)}), f32[32,2,128]{2,1,0:T(2,128)S(1)}, u32[]{:S(2)}, u32[]{:S(2)}) async-start(f32[32,2,128]{2,1,0:T(2,128)} %pair.1.after_ref), calls=%async_computation.1 | async-start | bytes 65536 | tf_op jit(solution)/shard_map/all_to_all | solution.py:368
  38.0 0.0 copy-start
  38.0 0.0 copy-start.1
  38.0 0.0 collective-permute-done.1.other_ref
  38.0 4.4 %smooth.1.smooth_ref = f32[512,128]{1,0:T(8,128)S(1)} custom-call(f32[1064,128]{1,0:T(8,128)S(1)} %merge.1.own_ref, f32[1064,128]{1,0:T(8,128)S(1)} %collective-permute-done.mate_ref, f32[1064,128]{1,0:T(8,128)S(1)} %collective-permute-done.1.other_ref, f32[32,2,128]{2,1,0:T(2,128)} %pair.1.after_ref), custom_call_target="tpu_custom_call" | custom-call | flops 20000000 | bytes 1929216 | tf_op jit(solution)/shard_map/smooth/pallas_call | solution.py:316
  42.4 4.3 %all-to-all-done.1 = f32[32,2,128]{2,1,0:T(2,128)S(1)} async-done(((f32[32,2,128]{2,1,0:T(2,128)}), f32[32,2,128]{2,1,0:T(2,128)S(1)}, u32[]{:S(2)}, u32[]{:S(2)}) %all-to-all-start.1) | async-done | bytes 32800 | tf_op jit(solution)/shard_map/all_to_all | solution.py:368
  46.7 0.0 copy-done
  46.7 0.0 copy-done.1
  46.7 1.5 %correct.1 = f32[512,128]{1,0:T(8,128)} custom-call(f32[64,128]{1,0:T(8,128)S(1)} %bitcast.23, f32[16,8192]{1,0:T(8,128)S(1)} %copy-done.1, s32[512,128]{1,0:T(8,128)S(1)} %bitcast.22, f32[512,128]{1,0:T(8,128)S(1)} %smooth.1.smooth_ref), custom_call_target="tpu_custom_call" | custom-call | bytes 1343488 | tf_op jit(solution)/shard_map/correct/pallas_call | solution.py:316
  (1 shorter events, 0.0 us)
Async XLA Ops:
  20.9 7.0 %collective-permute-start = (f32[1064,128]{1,0:T(8,128)S(1)}, f32[1064,128]{1,0:T(8,128)S(1)}, u32[]{:S(2)}, u32[]{:S(2)}) collective-permute-start(f32[1064,128]{1,0:T(8,128)S(1)} %merge.1.own_ref), channel_id=1, source_target_pairs={{0,8},{8,0},{16,24},{24,16},{32,40},{40,32},{48,56},{56,48},{64,72... | collective-permute-start | bytes 1634312 | tf_op jit(solution)/shard_map/ppermute | solution.py:362
  24.9 13.1 %collective-permute-start.1 = (f32[1064,128]{1,0:T(8,128)S(1)}, f32[1064,128]{1,0:T(8,128)S(1)}, u32[]{:S(2)}, u32[]{:S(2)}) collective-permute-start(f32[1064,128]{1,0:T(8,128)S(1)} %merge.1.own_ref), channel_id=1, source_target_pairs={{8,16},{16,8},{24,32},{32,24},{40,48},{48,40},{56,64},{64,56},{72,... | collective-permute-start | bytes 1634312 | tf_op jit(solution)/shard_map/ppermute | solution.py:363
  28.6 18.1 %all-to-all-start.1 = ((f32[32,2,128]{2,1,0:T(2,128)}), f32[32,2,128]{2,1,0:T(2,128)S(1)}, u32[]{:S(2)}, u32[]{:S(2)}) async-start(f32[32,2,128]{2,1,0:T(2,128)} %pair.1.after_ref), calls=%async_computation.1 | async-start | bytes 65536 | tf_op jit(solution)/shard_map/all_to_all | solution.py:368
  38.0 8.7 %copy-start = (s32[64,4,256]{2,1,0:T(4,128)S(1)}, s32[64,4,256]{2,1,0:T(4,128)}, u32[]{:S(2)}) copy-start(s32[64,4,256]{2,1,0:T(4,128)} %param.8) | copy-start | bytes 786436
  38.0 8.7 %copy-start.1 = (f32[16,8192]{1,0:T(8,128)S(1)}, f32[16,8192]{1,0:T(8,128)}, u32[]{:S(2)}) copy-start(f32[16,8192]{1,0:T(8,128)} %inverse_ref.1) | copy-start | bytes 1572868

commit v5 on v4

--- a/solution.py
+++ b/solution.py
@@ -22,7 +22,7 @@
 SUMS = 2 * ROWS + 2 * STRIP
 OWN = SUMS + 8
 FACE = 8
-CHUNKS = 4
+CHUNKS = 8
 NOTHING = 1e-30
 
 
@@ -44,16 +44,13 @@
     return split.transpose(0, 2, 1, 3).reshape(NZ, CX, TILES * LANES)
 
 
-def lane_table(entry, count):
-    lane = iota((8, LANES), 1)
-    table = jnp.zeros((8, LANES), jnp.float32)
-    for c in range(count):
-        table = jnp.where(lane == c, entry(c), table)
-    return table
-
-
-def pick(table, index):
-    return jnp.take_along_axis(table, index, axis=1, mode="promise_in_bounds")
+def pick(entries, index):
+    bit = 1
+    while len(entries) > 1:
+        odd = index & bit != 0
+        entries = [jnp.where(odd, entries[k + 1], entries[k]) for k in range(0, len(entries), 2)]
+        bit *= 2
+    return entries[0]
 
 
 def column_to_lanes(column, first):
@@ -65,13 +62,8 @@
     return ref[pl.ds(base + j * STEP + t * CX + x, 8, stride=FAR_ROW), :]
 
 
-def coarse_kernel(
-    perm_ref, residual_ref, support_ref, classes_ref, message_ref, own_ref,
-    support_buf, classes_buf, perm_buf, sems, perm_sem, classes_sem,
-):
+def coarse_kernel(residual_ref, support_ref, classes_ref, message_ref, own_ref, support_buf, classes_buf, sems):
     size = ROWS // CHUNKS
-    perm_copy = pltpu.make_async_copy(perm_ref, perm_buf, perm_sem)
-    classes_copy = pltpu.make_async_copy(classes_ref, classes_buf, classes_sem)
 
     def copies(k):
         at = pl.ds(k * size, size)
@@ -80,11 +72,15 @@
             pltpu.make_async_copy(support_ref.at[at, :], support_buf.at[at, :], sems.at[k, 1]),
         ]
 
-    perm_copy.start()
+    def classes_copy(k):
+        at = pl.ds(k * size, size)
+        return pltpu.make_async_copy(classes_ref.at[at, :], classes_buf.at[at, :], sems.at[k, 2])
+
     for k in range(CHUNKS):
         for copy in copies(k):
             copy.start()
-    classes_copy.start()
+    for k in range(CHUNKS):
+        classes_copy(k).start()
 
     def add(i, sums):
         value = own_ref[pl.ds(pl.multiple_of(ROWS + i * 8, 8), 8), :]
@@ -95,23 +91,25 @@
     for k in range(CHUNKS):
         for copy in copies(k):
             copy.wait()
-        sums = lax.fori_loop(k * size // 8, (k + 1) * size // 8, add, sums, unroll=4)
+        sums = lax.fori_loop(k * size // 8, (k + 1) * size // 8, add, sums, unroll=8)
+
+    def mark(i, carry):
+        at = pl.ds(pl.multiple_of(i * 8, 8), 8)
+        own_ref[at, :] = (classes_buf[at, :] + 1).astype(jnp.float32)
+        return carry
+
+    for k in range(CHUNKS):
+        classes_copy(k).wait()
+    lax.fori_loop(0, ROWS // 8, mark, 0, unroll=8)
+
     rows = jnp.concatenate([jnp.sum(s, axis=0, keepdims=True) for s in sums], axis=0)
     column = jnp.sum(rows, axis=1, keepdims=True)
     row = column_to_lanes(column, lax.axis_index("gy") * CF)
-
-    perm_copy.wait()
-    table = lane_table(lambda c: 1.0 / jnp.full((8, LANES), perm_buf[c]), perm_ref.shape[0])
-    classes_copy.wait()
-
-    def look_up(i, carry):
-        at = pl.ds(pl.multiple_of(i * 8, 8), 8)
-        own_ref[at, :] = pick(table, classes_buf[at, :])
-        return carry
-
-    lax.fori_loop(0, ROWS // 8, look_up, 0, unroll=8)
+    for k in range(message_ref.shape[0]):
+        message_ref[k, 0:FACE, :] = jnp.broadcast_to(row, (FACE, LANES))
 
     lane = iota((8, LANES), 1)
+    me = lax.axis_index("gy")
     for h in range(2):
         first = jnp.zeros((8, LANES), jnp.float32)
         final = jnp.zeros((8, LANES), jnp.float32)
@@ -124,11 +122,8 @@
                     both = pltpu.roll(both, shift, 1)
                 first = jnp.where(lane // 4 == shift // 4, both, first)
                 final = jnp.where((lane + 4) % LANES // 4 == shift // 4, both, final)
-        me = lax.axis_index("gy")
         for k in range(message_ref.shape[0]):
             message_ref[k, FACE + 8 * h : FACE + 8 * h + 8, :] = jnp.where(me < k, final, first)
-    for k in range(message_ref.shape[0]):
-        message_ref[k, 0:FACE, :] = jnp.broadcast_to(row, (FACE, LANES))
 
 
 def merge_kernel(got_ref, own_ref, out_ref):
@@ -154,7 +149,7 @@
 
 
 def smooth_kernel(
-    own_ref, mate_ref, other_ref, after_ref, out_ref,
+    perm_ref, own_ref, mate_ref, other_ref, after_ref, out_ref,
     res, upd, rem, inv, tx, ty, tyl, tz, tzu, flux, total,
 ):
     middle = 0.5 * (UPPER + LOWER)
@@ -167,28 +162,36 @@
     tiles = range(TILES + 1)
     groups = range(GROUPS)
 
+    table = [1.0 / jnp.full((8, LANES), perm_ref[c]) for c in range(perm_ref.shape[0])]
+
+    def resistivity(mark):
+        return jnp.where(mark > 0.0, pick(table, mark.astype(jnp.int32) - 1), NOTHING)
+
     odd = lax.axis_index("gx") % 2
     places = ((own_ref, DEPTH), (mate_ref, 2 * CX * (1 - odd)), (other_ref, 2 * CX * odd))
     for ref, place in places:
-        for x in range(CX):
+        strips = []
+        for n in range(2 * STRIP // 8):
+            strip = ref[pl.ds(2 * ROWS + 8 * n, 8), :]
+            marked = (lane + (4 if n >= STRIP // 8 else 0)) % 32 < 16
+            mark = jnp.where(marked, strip, 0.0)
+            strips.append(jnp.where(marked, resistivity(mark), 0.5 * strip))
+
+        def unpack(x, carry):
             i = place + x
             for j in groups:
                 for t in range(TILES):
-                    value = vector(ref, 0, t, x, j)
-                    res[i, t, j] = value if ref is own_ref else jnp.maximum(value, NOTHING)
+                    res[i, t, j] = resistivity(vector(ref, 0, t, x, j))
                     rem[i, t, j] = 0.5 * vector(ref, ROWS, t, x, j)
-                above = ref[pl.ds(2 * ROWS + j % 2 * 8, 8), :]
-                below = ref[pl.ds(2 * ROWS + STRIP + j % 2 * 8, 8), :]
-                for a in range(2):
+                above, below = strips[j % 2], strips[2 + j % 2]
+                for a, plane in enumerate((res, rem)):
                     shift = 32 * (j // 2) + 4 * (CX * a + x)
                     moved = jnp.where(lane // 4 == shift // 4, above, below)
-                    if shift:
-                        moved = pltpu.roll(moved, LANES - shift, 1)
-                    moved = jnp.where(halo, moved, 0.0)
-                    if a:
-                        rem[i, TILES, j] = 0.5 * moved
-                    else:
-                        res[i, TILES, j] = jnp.maximum(moved, NOTHING)
+                    moved = pltpu.roll(moved, (LANES - shift) % LANES, 1)
+                    plane[i, TILES, j] = jnp.where(halo, moved, 0.0 if a else NOTHING)
+            return carry
+
+        lax.fori_loop(0, CX, unpack, 0)
 
     def right(values):
         rolled = [pltpu.roll(v, LANES - 1, 1) for v in values]
@@ -288,8 +291,9 @@
     for q in range(gathered_ref.shape[0]):
         part = inverse_ref[:, q * LANES : (q + 1) * LANES] * gathered_ref[pl.ds(q, 1), :]
         sums[q % 4] = sums[q % 4] + part
-    column = jnp.sum((sums[0] + sums[1]) + (sums[2] + sums[3]), axis=1, keepdims=True)
-    table = jnp.broadcast_to(column_to_lanes(column, 0), (8, LANES))
+    total = (sums[0] + sums[1]) + (sums[2] + sums[3])
+    column = jnp.broadcast_to(jnp.sum(total, axis=1, keepdims=True), (CF, LANES))
+    table = [jnp.broadcast_to(column[c : c + 1, :], (8, LANES)) for c in range(CF)]
 
     def step(i, carry):
         at = pl.ds(pl.multiple_of(i * 8, 8), 8)
@@ -335,15 +339,12 @@
     message, own = call(
         coarse_kernel,
         [held(n_gy, FACE + STRIP, LANES), held(OWN, LANES)],
-        specs(pltpu.HBM, 4),
-        [class_perm, residual, support, classes],
+        specs(pltpu.HBM, 3),
+        [residual, support, classes],
         scratch_shapes=[
             pltpu.VMEM((ROWS, LANES), jnp.int32),
             pltpu.VMEM((ROWS, LANES), jnp.int32),
-            pltpu.SMEM(class_perm.shape, jnp.float32),
-            pltpu.SemaphoreType.DMA((CHUNKS, 2)),
-            pltpu.SemaphoreType.DMA,
-            pltpu.SemaphoreType.DMA,
+            pltpu.SemaphoreType.DMA((CHUNKS, 3)),
         ],
         limit=60,
         name="coarse",
@@ -372,8 +373,8 @@
     (smooth,) = call(
         smooth_kernel,
         [held(ROWS, LANES)],
-        specs(pltpu.VMEM, 3) + specs(pl.ANY),
-        [own, mate, other, rows],
+        specs(pltpu.SMEM) + specs(pltpu.VMEM, 3) + specs(pl.ANY),
+        [class_perm, own, mate, other, rows],
         flops=20_000_000,
         scratch_shapes=[planes] * 8
         + [

time: 48.4 us -> 47.3 us (0.977)
  waiting for transfers between devices: 4.3 us -> 2.7 us
    all_to_all x1, waiting for transfers between devices: 4.29 us -> 2.69 us  [local(): lax.all_to_all(rows, 'gx', 0, 0, axis_index_groups=groups, tiled=True)]
  transfers between devices with their start and end apart: 3 -> 3, of which waited for: 1 -> 1; matrix products, arithmetic and copies ran while one was open for 0% -> 0% of each run, Pallas kernels for 10% -> 14%
where the time goes in v5:
time: 47.3 us; the launch traced here: 47 us
  blocking collectives  18.3 us (39%)
  starting transfers between devices  16.5 us (35%)
  Pallas kernels  9.45 us (20%)
  waiting for transfers between devices  2.7 us (6%)
    all_to_all x1, blocking collectives, local(): got = lax.all_to_all(message, 'gy', 0, 0, tiled=True)  18.3 us
    all_to_all x1, starting transfers between devices, local(): lax.all_to_all(rows, 'gx', 0, 0, axis_index_groups=groups, tiled=True)  9.51 us
    pallas_call x5, Pallas kernels, call(): pl.pallas_call(kernel, out_shape=outs, in_specs=ins, out_specs=specs(out_...  9.45 us
    ppermute x1, starting transfers between devices, local(): mate = lax.ppermute(own, 'gx', pairs)  3.97 us
    ppermute x1, starting transfers between devices, local(): other = lax.ppermute(own, 'gx', others)  3.02 us
    all_to_all x1, waiting for transfers between devices, local(): lax.all_to_all(rows, 'gx', 0, 0, axis_index_groups=groups, tiled=True)  2.69 us
  transfers between devices with their start and end apart: 3, of which 1 were waited for; matrix products, arithmetic and copies ran while one was open for 0% of the time, Pallas kernels for 14%

profile of v5, /device:TPU:1, one launch (start us, length us, event | category | flops | bytes accessed | tf_op | source)
XLA Modules:
  0.0 47.0 jit_solution(2101587641679968370)
XLA Ops:
  0.0 1.8 %coarse.1 = (f32[8,24,128]{2,1,0:T(8,128)S(1)}, f32[1064,128]{1,0:T(8,128)S(1)}) custom-call(f32[512,128]{1,0:T(8,128)} %bitcast.24, s32[512,128]{1,0:T(8,128)} %bitcast.21, s32[512,128]{1,0:T(8,128)} %bitcast.25), custom_call_target="tpu_custom_call" | custom-call | bytes 1429504 | tf_op jit(solution)/shard_map/coarse/pallas_call | solution.py:320
  1.8 18.3 %all_to_all.10.got_ref = f32[8,24,128]{2,1,0:T(8,128)S(1)} all-to-all(f32[8,24,128]{2,1,0:T(8,128)S(1)} %get-tuple-element.7), channel_id=1, replica_groups=mesh['gx'=64,'gy'=8] {'gy'}, dimensions={0} | all-to-all | bytes 196608 | tf_op jit(solution)/shard_map/all_to_all | solution.py:352
  20.1 4.0 %collective-permute-start = (f32[1064,128]{1,0:T(8,128)S(1)}, f32[1064,128]{1,0:T(8,128)S(1)}, u32[]{:S(2)}, u32[]{:S(2)}) collective-permute-start(f32[1064,128]{1,0:T(8,128)S(1)} %merge.1.own_ref), channel_id=1, source_target_pairs={{0,8},{8,0},{16,24},{24,16},{32,40},{40,32},{48,56},{56,48},{64,72... | collective-permute-start | bytes 1634312 | tf_op jit(solution)/shard_map/ppermute | solution.py:363
  24.1 3.0 %collective-permute-start.1 = (f32[1064,128]{1,0:T(8,128)S(1)}, f32[1064,128]{1,0:T(8,128)S(1)}, u32[]{:S(2)}, u32[]{:S(2)}) collective-permute-start(f32[1064,128]{1,0:T(8,128)S(1)} %merge.1.own_ref), channel_id=1, source_target_pairs={{8,16},{16,8},{24,32},{32,24},{40,48},{48,40},{56,64},{64,56},{72,... | collective-permute-start | bytes 1634312 | tf_op jit(solution)/shard_map/ppermute | solution.py:364
  27.1 0.0 collective-permute-done.mate_ref
  27.1 0.6 %pair.1.after_ref = f32[32,2,128]{2,1,0:T(2,128)} custom-call(f32[1064,128]{1,0:T(8,128)S(1)} %merge.1.own_ref, f32[1064,128]{1,0:T(8,128)S(1)} %collective-permute-done.mate_ref), custom_call_target="tpu_custom_call" | custom-call | bytes 1122304 | tf_op jit(solution)/shard_map/pair/pallas_call | solution.py:320
  27.8 0.0 copy-start.2
  27.8 9.5 %all-to-all-start.1 = ((f32[32,2,128]{2,1,0:T(2,128)}), f32[32,2,128]{2,1,0:T(2,128)S(1)}, u32[]{:S(2)}, u32[]{:S(2)}) async-start(f32[32,2,128]{2,1,0:T(2,128)} %pair.1.after_ref), calls=%async_computation.1 | async-start | bytes 65536 | tf_op jit(solution)/shard_map/all_to_all | solution.py:369
  37.3 0.0 copy-start
  37.3 0.0 copy-start.1
  37.3 0.0 collective-permute-done.1.other_ref
  37.3 0.0 copy-done.2
  37.3 6.0 %smooth.1.smooth_ref = f32[512,128]{1,0:T(8,128)S(1)} custom-call(f32[16]{0:T(128)S(1)} %copy-done.2, f32[1064,128]{1,0:T(8,128)S(1)} %merge.1.own_ref, f32[1064,128]{1,0:T(8,128)S(1)} %collective-permute-done.mate_ref, f32[1064,128]{1,0:T(8,128)S(1)} %collective-permute-done.1.other_ref, f32[32,2,128]{2,1,0:T(2,128)} %pair.1.after_ref), custom_call_target="tpu_custom_call" | custom-call | flops 20000000 | bytes 1929280 | tf_op jit(solution)/shard_map/smooth/pallas_call | solution.py:320
  43.3 2.7 %all-to-all-done.1 = f32[32,2,128]{2,1,0:T(2,128)S(1)} async-done(((f32[32,2,128]{2,1,0:T(2,128)}), f32[32,2,128]{2,1,0:T(2,128)S(1)}, u32[]{:S(2)}, u32[]{:S(2)}) %all-to-all-start.1) | async-done | bytes 32800 | tf_op jit(solution)/shard_map/all_to_all | solution.py:369
  46.0 0.0 copy-done
  46.0 0.0 copy-done.1
  46.0 1.0 %correct.1 = f32[512,128]{1,0:T(8,128)} custom-call(f32[64,128]{1,0:T(8,128)S(1)} %bitcast.23, f32[16,8192]{1,0:T(8,128)S(1)} %copy-done.1, s32[512,128]{1,0:T(8,128)S(1)} %bitcast.22, f32[512,128]{1,0:T(8,128)S(1)} %smooth.1.smooth_ref), custom_call_target="tpu_custom_call" | custom-call | bytes 1343488 | tf_op jit(solution)/shard_map/correct/pallas_call | solution.py:320
  (1 shorter events, 0.0 us)
Async XLA Ops:
  20.1 7.0 %collective-permute-start = (f32[1064,128]{1,0:T(8,128)S(1)}, f32[1064,128]{1,0:T(8,128)S(1)}, u32[]{:S(2)}, u32[]{:S(2)}) collective-permute-start(f32[1064,128]{1,0:T(8,128)S(1)} %merge.1.own_ref), channel_id=1, source_target_pairs={{0,8},{8,0},{16,24},{24,16},{32,40},{40,32},{48,56},{56,48},{64,72... | collective-permute-start | bytes 1634312 | tf_op jit(solution)/shard_map/ppermute | solution.py:363
  24.1 13.2 %collective-permute-start.1 = (f32[1064,128]{1,0:T(8,128)S(1)}, f32[1064,128]{1,0:T(8,128)S(1)}, u32[]{:S(2)}, u32[]{:S(2)}) collective-permute-start(f32[1064,128]{1,0:T(8,128)S(1)} %merge.1.own_ref), channel_id=1, source_target_pairs={{8,16},{16,8},{24,32},{32,24},{40,48},{48,40},{56,64},{64,56},{72,... | collective-permute-start | bytes 1634312 | tf_op jit(solution)/shard_map/ppermute | solution.py:364
  27.8 9.6 %copy-start.2 = (f32[16]{0:T(128)S(1)}, f32[16]{0:T(128)}, u32[]{:S(2)}) copy-start(f32[16]{0:T(128)} %perm_ref.1) | copy-start | bytes 196
  27.8 18.2 %all-to-all-start.1 = ((f32[32,2,128]{2,1,0:T(2,128)}), f32[32,2,128]{2,1,0:T(2,128)S(1)}, u32[]{:S(2)}, u32[]{:S(2)}) async-start(f32[32,2,128]{2,1,0:T(2,128)} %pair.1.after_ref), calls=%async_computation.1 | async-start | bytes 65536 | tf_op jit(solution)/shard_map/all_to_all | solution.py:369
  37.3 8.7 %copy-start = (s32[64,4,256]{2,1,0:T(4,128)S(1)}, s32[64,4,256]{2,1,0:T(4,128)}, u32[]{:S(2)}) copy-start(s32[64,4,256]{2,1,0:T(4,128)} %param.8) | copy-start | bytes 786436
  37.3 8.7 %copy-start.1 = (f32[16,8192]{1,0:T(8,128)S(1)}, f32[16,8192]{1,0:T(8,128)}, u32[]{:S(2)}) copy-start(f32[16,8192]{1,0:T(8,128)} %inverse_ref.1) | copy-start | bytes 1572868

commit v6 on v5

--- a/solution.py
+++ b/solution.py
@@ -22,6 +22,7 @@
 SUMS = 2 * ROWS + 2 * STRIP
 OWN = SUMS + 8
 FACE = 8
+TURN_Y, TURN_X = 4, 32
 CHUNKS = 8
 NOTHING = 1e-30
 
@@ -42,6 +43,10 @@
 def block_of(rows):
     split = rows.reshape(NZ, TILES, CX, LANES)
     return split.transpose(0, 2, 1, 3).reshape(NZ, CX, TILES * LANES)
+
+
+def turned(place, turn, count):
+    return (place + turn + count) % count
 
 
 def pick(entries, index):
@@ -110,6 +115,7 @@
 
     lane = iota((8, LANES), 1)
     me = lax.axis_index("gy")
+    count = message_ref.shape[0]
     for h in range(2):
         first = jnp.zeros((8, LANES), jnp.float32)
         final = jnp.zeros((8, LANES), jnp.float32)
@@ -123,15 +129,15 @@
                 first = jnp.where(lane // 4 == shift // 4, both, first)
                 final = jnp.where((lane + 4) % LANES // 4 == shift // 4, both, final)
         for k in range(message_ref.shape[0]):
-            message_ref[k, FACE + 8 * h : FACE + 8 * h + 8, :] = jnp.where(me < k, final, first)
+            message_ref[k, FACE + 8 * h : FACE + 8 * h + 8, :] = jnp.where(me < turned(k, TURN_Y, count), final, first)
 
 
 def merge_kernel(got_ref, own_ref, out_ref):
     count = got_ref.shape[0]
     me = lax.axis_index("gy")
     strip = pl.ds(FACE, STRIP)
-    above = got_ref[jnp.minimum(me + 1, count - 1), strip, :]
-    below = got_ref[jnp.maximum(me - 1, 0), strip, :]
+    above = got_ref[turned(me + 1, -TURN_Y, count), strip, :]
+    below = got_ref[turned(me - 1, -TURN_Y, count), strip, :]
     out_ref[pl.ds(2 * ROWS, STRIP), :] = jnp.where(me < count - 1, above, 0.0)
     out_ref[pl.ds(2 * ROWS + STRIP, STRIP), :] = jnp.where(me > 0, below, 0.0)
     row = got_ref[0, 0:8, :]
@@ -150,7 +156,7 @@
 
 def smooth_kernel(
     perm_ref, own_ref, mate_ref, other_ref, after_ref, out_ref,
-    res, upd, rem, inv, tx, ty, tyl, tz, tzu, flux, total,
+    perm_buf, sem, res, upd, rem, inv, tx, ty, tyl, tz, tzu, flux, total,
 ):
     middle = 0.5 * (UPPER + LOWER)
     spread = 0.5 * (UPPER - LOWER)
@@ -162,36 +168,42 @@
     tiles = range(TILES + 1)
     groups = range(GROUPS)
 
-    table = [1.0 / jnp.full((8, LANES), perm_ref[c]) for c in range(perm_ref.shape[0])]
-
-    def resistivity(mark):
-        return jnp.where(mark > 0.0, pick(table, mark.astype(jnp.int32) - 1), NOTHING)
-
+    perm_copy = pltpu.make_async_copy(perm_ref, perm_buf, sem)
+    perm_copy.start()
     odd = lax.axis_index("gx") % 2
     places = ((own_ref, DEPTH), (mate_ref, 2 * CX * (1 - odd)), (other_ref, 2 * CX * odd))
-    for ref, place in places:
+
+    def unpack(ref, place, plane, a, change, outside):
+        def one(x, carry):
+            for j in groups:
+                for t in range(TILES):
+                    plane[place + x, t, j] = change(vector(ref, a * ROWS, t, x, j))
+            return carry
+
+        lax.fori_loop(0, CX, one, 0, unroll=2)
         strips = []
         for n in range(2 * STRIP // 8):
             strip = ref[pl.ds(2 * ROWS + 8 * n, 8), :]
             marked = (lane + (4 if n >= STRIP // 8 else 0)) % 32 < 16
-            mark = jnp.where(marked, strip, 0.0)
-            strips.append(jnp.where(marked, resistivity(mark), 0.5 * strip))
-
-        def unpack(x, carry):
-            i = place + x
+            strips.append(change(jnp.where(marked, 0.0, strip) if a else jnp.where(marked, strip, 0.0)))
+        for x in range(CX):
             for j in groups:
-                for t in range(TILES):
-                    res[i, t, j] = resistivity(vector(ref, 0, t, x, j))
-                    rem[i, t, j] = 0.5 * vector(ref, ROWS, t, x, j)
-                above, below = strips[j % 2], strips[2 + j % 2]
-                for a, plane in enumerate((res, rem)):
-                    shift = 32 * (j // 2) + 4 * (CX * a + x)
-                    moved = jnp.where(lane // 4 == shift // 4, above, below)
-                    moved = pltpu.roll(moved, (LANES - shift) % LANES, 1)
-                    plane[i, TILES, j] = jnp.where(halo, moved, 0.0 if a else NOTHING)
-            return carry
-
-        lax.fori_loop(0, CX, unpack, 0)
+                shift = 32 * (j // 2) + 4 * (CX * a + x)
+                moved = jnp.where(lane // 4 == shift // 4, strips[j % 2], strips[2 + j % 2])
+                if shift:
+                    moved = pltpu.roll(moved, LANES - shift, 1)
+                plane[place + x, TILES, j] = jnp.where(halo, moved, outside)
+
+    for ref, place in places:
+        unpack(ref, place, rem, 1, lambda value: 0.5 * value, 0.0)
+    perm_copy.wait()
+    table = [1.0 / jnp.full((8, LANES), perm_buf[c]) for c in range(perm_ref.shape[0])]
+
+    def resistivity(mark):
+        return jnp.where(mark > 0.0, pick(table, mark.astype(jnp.int32) - 1), NOTHING)
+
+    for ref, place in places:
+        unpack(ref, place, res, 0, resistivity, NOTHING)
 
     def right(values):
         rolled = [pltpu.roll(v, LANES - 1, 1) for v in values]
@@ -288,8 +300,10 @@
 def correct_kernel(gathered_ref, inverse_ref, support_ref, smooth_ref, out_ref, buf, sems):
     zero = jnp.zeros((CF, LANES), jnp.float32)
     sums = [zero] * 4
-    for q in range(gathered_ref.shape[0]):
-        part = inverse_ref[:, q * LANES : (q + 1) * LANES] * gathered_ref[pl.ds(q, 1), :]
+    count = gathered_ref.shape[0]
+    for q in range(count):
+        row = gathered_ref[pl.ds(turned(q, -TURN_X, count), 1), :]
+        part = inverse_ref[:, q * LANES : (q + 1) * LANES] * row
         sums[q % 4] = sums[q % 4] + part
     total = (sums[0] + sums[1]) + (sums[2] + sums[3])
     column = jnp.broadcast_to(jnp.sum(total, axis=1, keepdims=True), (CF, LANES))
@@ -349,7 +363,8 @@
         limit=60,
         name="coarse",
     )
-    got = lax.all_to_all(message, "gy", 0, 0, tiled=True)
+    columns = [[turned(k, TURN_Y, n_gy) for k in range(n_gy)]]
+    got = lax.all_to_all(message, "gy", 0, 0, axis_index_groups=columns, tiled=True)
     (own,) = call(
         merge_kernel,
         [held(OWN, LANES)],
@@ -365,7 +380,7 @@
     (rows,) = call(
         pair_kernel, [held(n_gx // 2, 2, LANES)], specs(pltpu.VMEM, 2), [own, mate], name="pair"
     )
-    groups = [list(range(k, n_gx, 2)) for k in range(2)]
+    groups = [[turned(2 * i, TURN_X, n_gx) + k for i in range(n_gx // 2)] for k in range(2)]
     gathered = lax.all_to_all(rows, "gx", 0, 0, axis_index_groups=groups, tiled=True)
     gathered = gathered.reshape(n_gx, LANES)
 
@@ -373,10 +388,11 @@
     (smooth,) = call(
         smooth_kernel,
         [held(ROWS, LANES)],
-        specs(pltpu.SMEM) + specs(pltpu.VMEM, 3) + specs(pl.ANY),
+        specs(pltpu.HBM) + specs(pltpu.VMEM, 3) + specs(pl.ANY),
         [class_perm, own, mate, other, rows],
         flops=20_000_000,
-        scratch_shapes=[planes] * 8
+        scratch_shapes=[pltpu.SMEM(class_perm.shape, jnp.float32), pltpu.SemaphoreType.DMA]
+        + [planes] * 8
         + [
             pltpu.VMEM((WIDE, TILES + 1, 8, LANES), jnp.float32),
             pltpu.VMEM((TILES + 1, GROUPS, 8, LANES), jnp.float32),

time: 47.3 us -> 43 us (0.909)
  waiting for transfers between devices: 2.7 us -> 0.01 us
  blocking collectives: 18.3 us -> 16.4 us
  starting transfers between devices: 16.5 us -> 17.4 us
  Pallas kernels: 9.45 us -> 8.82 us
    all_to_all x1, waiting for transfers between devices: 2.69 us -> 0.01 us  [local(): lax.all_to_all(rows, 'gx', 0, 0, axis_index_groups=groups, tiled=True)]
    all_to_all x1, blocking collectives: 18.3 us -> 16.4 us  [local(): lax.all_to_all(message, 'gy', 0, 0, axis_index_groups=columns, tiled=True)]
    all_to_all x1, starting transfers between devices: 9.51 us -> 10.7 us  [local(): lax.all_to_all(rows, 'gx', 0, 0, axis_index_groups=groups, tiled=True)]
    pallas_call x5, Pallas kernels: 9.45 us -> 8.82 us  [call(): pl.pallas_call(kernel, out_shape=outs, in_specs=ins, out_specs=specs(out_...]
  transfers between devices with their start and end apart: 3 -> 3, of which waited for: 1 -> 0; matrix products, arithmetic and copies ran while one was open for 0% -> 0% of each run, Pallas kernels for 14% -> 14%
where the time goes in v6:
time: 43 us; the launch traced here: 42.7 us
  starting transfers between devices  17.4 us (40%)
  blocking collectives  16.4 us (38%)
  Pallas kernels  8.82 us (21%)
    all_to_all x1, blocking collectives, local(): lax.all_to_all(message, 'gy', 0, 0, axis_index_groups=columns, tiled=True)  16.4 us
    all_to_all x1, starting transfers between devices, local(): lax.all_to_all(rows, 'gx', 0, 0, axis_index_groups=groups, tiled=True)  10.7 us
    pallas_call x5, Pallas kernels, call(): pl.pallas_call(kernel, out_shape=outs, in_specs=ins, out_specs=specs(out_...  8.82 us
    ppermute x1, starting transfers between devices, local(): mate = lax.ppermute(own, 'gx', pairs)  3.65 us
    ppermute x1, starting transfers between devices, local(): other = lax.ppermute(own, 'gx', others)  3.02 us
  transfers between devices with their start and end apart: 3, of which 0 were waited for; matrix products, arithmetic and copies ran while one was open for 0% of the time, Pallas kernels for 14%

profile of v6, /device:TPU:1, one launch (start us, length us, event | category | flops | bytes accessed | tf_op | source)
XLA Modules:
  0.0 42.7 jit_solution(14199515793031295128)
XLA Ops:
  0.0 1.8 %coarse.1 = (f32[8,24,128]{2,1,0:T(8,128)S(1)}, f32[1064,128]{1,0:T(8,128)S(1)}) custom-call(f32[512,128]{1,0:T(8,128)} %bitcast.24, s32[512,128]{1,0:T(8,128)} %bitcast.21, s32[512,128]{1,0:T(8,128)} %bitcast.25), custom_call_target="tpu_custom_call" | custom-call | bytes 1429504 | tf_op jit(solution)/shard_map/coarse/pallas_call | solution.py:334
  1.8 16.4 %all_to_all.10.got_ref = f32[8,24,128]{2,1,0:T(8,128)S(1)} all-to-all(f32[8,24,128]{2,1,0:T(8,128)S(1)} %get-tuple-element.7), channel_id=1, replica_groups={{4,5,6,7,0,1,2,3},{12,13,14,15,8,9,10,11},{20,21,22,23,16,17,18,19},{28..., dimensions={0} | all-to-all | bytes 196608 | tf_op jit(solution)/shard_map/all_to_all | solution.py:367
  18.2 3.6 %collective-permute-start = (f32[1064,128]{1,0:T(8,128)S(1)}, f32[1064,128]{1,0:T(8,128)S(1)}, u32[]{:S(2)}, u32[]{:S(2)}) collective-permute-start(f32[1064,128]{1,0:T(8,128)S(1)} %merge.1.own_ref), channel_id=1, source_target_pairs={{0,8},{8,0},{16,24},{24,16},{32,40},{40,32},{48,56},{56,48},{64,72... | collective-permute-start | bytes 1634312 | tf_op jit(solution)/shard_map/ppermute | solution.py:378
  21.9 3.0 %collective-permute-start.1 = (f32[1064,128]{1,0:T(8,128)S(1)}, f32[1064,128]{1,0:T(8,128)S(1)}, u32[]{:S(2)}, u32[]{:S(2)}) collective-permute-start(f32[1064,128]{1,0:T(8,128)S(1)} %merge.1.own_ref), channel_id=1, source_target_pairs={{8,16},{16,8},{24,32},{32,24},{40,48},{48,40},{56,64},{64,56},{72,... | collective-permute-start | bytes 1634312 | tf_op jit(solution)/shard_map/ppermute | solution.py:379
  24.9 0.0 collective-permute-done.mate_ref
  24.9 0.6 %pair.1.after_ref = f32[32,2,128]{2,1,0:T(2,128)} custom-call(f32[1064,128]{1,0:T(8,128)S(1)} %merge.1.own_ref, f32[1064,128]{1,0:T(8,128)S(1)} %collective-permute-done.mate_ref), custom_call_target="tpu_custom_call" | custom-call | bytes 1122304 | tf_op jit(solution)/shard_map/pair/pallas_call | solution.py:334
  25.5 0.0 copy-start.2
  25.5 10.7 %all-to-all-start.1 = ((f32[32,2,128]{2,1,0:T(2,128)}), f32[32,2,128]{2,1,0:T(2,128)S(1)}, u32[]{:S(2)}, u32[]{:S(2)}) async-start(f32[32,2,128]{2,1,0:T(2,128)} %pair.1.after_ref), calls=%async_computation.1 | async-start | bytes 65536 | tf_op jit(solution)/shard_map/all_to_all | solution.py:384
  36.2 0.0 copy-start
  36.3 0.0 copy-start.1
  36.3 0.0 collective-permute-done.1.other_ref
  36.3 0.0 copy-done.2
  36.3 5.3 %smooth.1.smooth_ref = f32[512,128]{1,0:T(8,128)S(1)} custom-call(f32[16]{0:T(128)S(1)} %copy-done.2, f32[1064,128]{1,0:T(8,128)S(1)} %merge.1.own_ref, f32[1064,128]{1,0:T(8,128)S(1)} %collective-permute-done.mate_ref, f32[1064,128]{1,0:T(8,128)S(1)} %collective-permute-done.1.other_ref, f32[32,2,128]{2,1,0:T(2,128)} %pair.1.after_ref), custom_call_target="tpu_custom_call" | custom-call | flops 20000000 | bytes 1929280 | tf_op jit(solution)/shard_map/smooth/pallas_call | solution.py:334
  41.6 0.0 all-to-all-done.1
  41.6 0.0 copy-done
  41.6 0.0 copy-done.1
  41.7 1.0 %correct.1 = f32[512,128]{1,0:T(8,128)} custom-call(f32[64,128]{1,0:T(8,128)S(1)} %bitcast.23, f32[16,8192]{1,0:T(8,128)S(1)} %copy-done.1, s32[512,128]{1,0:T(8,128)S(1)} %bitcast.22, f32[512,128]{1,0:T(8,128)S(1)} %smooth.1.smooth_ref), custom_call_target="tpu_custom_call" | custom-call | bytes 1343488 | tf_op jit(solution)/shard_map/correct/pallas_call | solution.py:334
  (1 shorter events, 0.0 us)
Async XLA Ops:
  18.2 6.7 %collective-permute-start = (f32[1064,128]{1,0:T(8,128)S(1)}, f32[1064,128]{1,0:T(8,128)S(1)}, u32[]{:S(2)}, u32[]{:S(2)}) collective-permute-start(f32[1064,128]{1,0:T(8,128)S(1)} %merge.1.own_ref), channel_id=1, source_target_pairs={{0,8},{8,0},{16,24},{24,16},{32,40},{40,32},{48,56},{56,48},{64,72... | collective-permute-start | bytes 1634312 | tf_op jit(solution)/shard_map/ppermute | solution.py:378
  21.9 14.4 %collective-permute-start.1 = (f32[1064,128]{1,0:T(8,128)S(1)}, f32[1064,128]{1,0:T(8,128)S(1)}, u32[]{:S(2)}, u32[]{:S(2)}) collective-permute-start(f32[1064,128]{1,0:T(8,128)S(1)} %merge.1.own_ref), channel_id=1, source_target_pairs={{8,16},{16,8},{24,32},{32,24},{40,48},{48,40},{56,64},{64,56},{72,... | collective-permute-start | bytes 1634312 | tf_op jit(solution)/shard_map/ppermute | solution.py:379
  25.5 10.7 %copy-start.2 = (f32[16]{0:T(128)S(1)}, f32[16]{0:T(128)}, u32[]{:S(2)}) copy-start(f32[16]{0:T(128)} %perm_ref.1) | copy-start | bytes 196
  25.5 16.1 %all-to-all-start.1 = ((f32[32,2,128]{2,1,0:T(2,128)}), f32[32,2,128]{2,1,0:T(2,128)S(1)}, u32[]{:S(2)}, u32[]{:S(2)}) async-start(f32[32,2,128]{2,1,0:T(2,128)} %pair.1.after_ref), calls=%async_computation.1 | async-start | bytes 65536 | tf_op jit(solution)/shard_map/all_to_all | solution.py:384
  36.2 5.4 %copy-start = (s32[64,4,256]{2,1,0:T(4,128)S(1)}, s32[64,4,256]{2,1,0:T(4,128)}, u32[]{:S(2)}) copy-start(s32[64,4,256]{2,1,0:T(4,128)} %param.8) | copy-start | bytes 786436
  36.3 5.4 %copy-start.1 = (f32[16,8192]{1,0:T(8,128)S(1)}, f32[16,8192]{1,0:T(8,128)}, u32[]{:S(2)}) copy-start(f32[16,8192]{1,0:T(8,128)} %inverse_ref.1) | copy-start | bytes 1572868

commit v7 on v5

--- a/solution.py
+++ b/solution.py
@@ -21,7 +21,8 @@
 STRIP = 16
 SUMS = 2 * ROWS + 2 * STRIP
 OWN = SUMS + 8
-FACE = 8
+SPARE = 96
+TURN_Y, TURN_X = 4, 32
 CHUNKS = 8
 NOTHING = 1e-30
 
@@ -42,6 +43,14 @@
 def block_of(rows):
     split = rows.reshape(NZ, TILES, CX, LANES)
     return split.transpose(0, 2, 1, 3).reshape(NZ, CX, TILES * LANES)
+
+
+def within(lane, first, count):
+    return (lane >= first) & (lane < first + count)
+
+
+def turned(place, turn, count):
+    return (place + turn + count) % count
 
 
 def pick(entries, index):
@@ -62,7 +71,10 @@
     return ref[pl.ds(base + j * STEP + t * CX + x, 8, stride=FAR_ROW), :]
 
 
-def coarse_kernel(residual_ref, support_ref, classes_ref, message_ref, own_ref, support_buf, classes_buf, sems):
+def coarse_kernel(
+    perm_ref, residual_ref, support_ref, classes_ref, message_ref, own_ref,
+    perm_buf, support_buf, classes_buf, perm_sem, sems,
+):
     size = ROWS // CHUNKS
 
     def copies(k):
@@ -76,6 +88,8 @@
         at = pl.ds(k * size, size)
         return pltpu.make_async_copy(classes_ref.at[at, :], classes_buf.at[at, :], sems.at[k, 2])
 
+    perm_copy = pltpu.make_async_copy(perm_ref, perm_buf, perm_sem)
+    perm_copy.start()
     for k in range(CHUNKS):
         for copy in copies(k):
             copy.start()
@@ -93,50 +107,56 @@
             copy.wait()
         sums = lax.fori_loop(k * size // 8, (k + 1) * size // 8, add, sums, unroll=8)
 
-    def mark(i, carry):
+    perm_copy.wait()
+    table = [1.0 / jnp.full((8, LANES), perm_buf[c]) for c in range(perm_ref.shape[0])]
+
+    def look_up(i, carry):
         at = pl.ds(pl.multiple_of(i * 8, 8), 8)
-        own_ref[at, :] = (classes_buf[at, :] + 1).astype(jnp.float32)
+        own_ref[at, :] = pick(table, classes_buf[at, :])
         return carry
 
     for k in range(CHUNKS):
         classes_copy(k).wait()
-    lax.fori_loop(0, ROWS // 8, mark, 0, unroll=8)
+    lax.fori_loop(0, ROWS // 8, look_up, 0, unroll=4)
 
     rows = jnp.concatenate([jnp.sum(s, axis=0, keepdims=True) for s in sums], axis=0)
     column = jnp.sum(rows, axis=1, keepdims=True)
-    row = column_to_lanes(column, lax.axis_index("gy") * CF)
-    for k in range(message_ref.shape[0]):
-        message_ref[k, 0:FACE, :] = jnp.broadcast_to(row, (FACE, LANES))
+    row = column_to_lanes(column, SPARE)
 
     lane = iota((8, LANES), 1)
     me = lax.axis_index("gy")
-    for h in range(2):
-        first = jnp.zeros((8, LANES), jnp.float32)
-        final = jnp.zeros((8, LANES), jnp.float32)
-        for g in range(GROUPS // 2):
-            for item in range(2 * CX):
-                low, high = (vector(own_ref, item // CX * ROWS, t, item % CX, 2 * g + h) for t in range(2))
-                both = jnp.where(lane < 64, low, high)
-                shift = 32 * g + 4 * item
+    count = message_ref.shape[0]
+    for a in range(2):
+        width = DEPTH - a
+        first = final = jnp.zeros((8, LANES), jnp.float32)
+        for j in range(GROUPS):
+            for x in range(CX):
+                both = jnp.where(lane < 64, vector(own_ref, a * ROWS, 0, x, j), vector(own_ref, a * ROWS, 1, x, j))
+                shift = width * (CX * j + x)
                 if shift:
                     both = pltpu.roll(both, shift, 1)
-                first = jnp.where(lane // 4 == shift // 4, both, first)
-                final = jnp.where((lane + 4) % LANES // 4 == shift // 4, both, final)
-        for k in range(message_ref.shape[0]):
-            message_ref[k, FACE + 8 * h : FACE + 8 * h + 8, :] = jnp.where(me < k, final, first)
+                first = jnp.where(within(lane, shift, width), both, first)
+                final = jnp.where(within(lane, (shift - width) % LANES, width), both, final)
+        for k in range(count):
+            strip = jnp.where(me < turned(k, TURN_Y, count), final, first)
+            if a:
+                strip = jnp.where(within(lane, SPARE, CF), row, strip)
+            message_ref[k, 8 * a : 8 * a + 8, :] = strip
 
 
 def merge_kernel(got_ref, own_ref, out_ref):
     count = got_ref.shape[0]
     me = lax.axis_index("gy")
-    strip = pl.ds(FACE, STRIP)
-    above = got_ref[jnp.minimum(me + 1, count - 1), strip, :]
-    below = got_ref[jnp.maximum(me - 1, 0), strip, :]
+    above = got_ref[turned(me + 1, -TURN_Y, count)]
+    below = got_ref[turned(me - 1, -TURN_Y, count)]
     out_ref[pl.ds(2 * ROWS, STRIP), :] = jnp.where(me < count - 1, above, 0.0)
     out_ref[pl.ds(2 * ROWS + STRIP, STRIP), :] = jnp.where(me > 0, below, 0.0)
-    row = got_ref[0, 0:8, :]
-    for k in range(1, count):
-        row = row + got_ref[k, 0:8, :]
+    lane = iota((8, LANES), 1)
+    row = jnp.zeros((8, LANES), jnp.float32)
+    for k in range(count):
+        first = CF * turned(k, TURN_Y, count)
+        moved = pltpu.roll(got_ref[k, 8:16, :], (first - SPARE) % LANES, 1) if first != SPARE else got_ref[k, 8:16, :]
+        row = jnp.where(within(lane, first, CF), moved, row)
     out_ref[pl.ds(SUMS, 8), :] = row
 
 
@@ -149,49 +169,40 @@
 
 
 def smooth_kernel(
-    perm_ref, own_ref, mate_ref, other_ref, after_ref, out_ref,
+    own_ref, mate_ref, other_ref, after_ref, out_ref,
     res, upd, rem, inv, tx, ty, tyl, tz, tzu, flux, total,
 ):
     middle = 0.5 * (UPPER + LOWER)
     spread = 0.5 * (UPPER - LOWER)
     sigma = middle / spread
     lane = iota((8, LANES), 1)
-    low_lane = lane < 4
-    halo = low_lane | (lane >= LANES - 4)
     top, bottom = iota((8, LANES), 0) == 0, iota((8, LANES), 0) == 7
     tiles = range(TILES + 1)
     groups = range(GROUPS)
 
-    table = [1.0 / jnp.full((8, LANES), perm_ref[c]) for c in range(perm_ref.shape[0])]
-
-    def resistivity(mark):
-        return jnp.where(mark > 0.0, pick(table, mark.astype(jnp.int32) - 1), NOTHING)
-
     odd = lax.axis_index("gx") % 2
     places = ((own_ref, DEPTH), (mate_ref, 2 * CX * (1 - odd)), (other_ref, 2 * CX * odd))
+
     for ref, place in places:
-        strips = []
-        for n in range(2 * STRIP // 8):
-            strip = ref[pl.ds(2 * ROWS + 8 * n, 8), :]
-            marked = (lane + (4 if n >= STRIP // 8 else 0)) % 32 < 16
-            mark = jnp.where(marked, strip, 0.0)
-            strips.append(jnp.where(marked, resistivity(mark), 0.5 * strip))
-
-        def unpack(x, carry):
+        faces = [[ref[pl.ds(2 * ROWS + 8 * n, 8), :] for n in (a, a + 2)] for a in range(2)]
+        for x in range(CX):
             i = place + x
             for j in groups:
                 for t in range(TILES):
-                    res[i, t, j] = resistivity(vector(ref, 0, t, x, j))
+                    value = vector(ref, 0, t, x, j)
+                    res[i, t, j] = value if ref is own_ref else jnp.maximum(value, NOTHING)
                     rem[i, t, j] = 0.5 * vector(ref, ROWS, t, x, j)
-                above, below = strips[j % 2], strips[2 + j % 2]
-                for a, plane in enumerate((res, rem)):
-                    shift = 32 * (j // 2) + 4 * (CX * a + x)
-                    moved = jnp.where(lane // 4 == shift // 4, above, below)
-                    moved = pltpu.roll(moved, (LANES - shift) % LANES, 1)
-                    plane[i, TILES, j] = jnp.where(halo, moved, 0.0 if a else NOTHING)
-            return carry
-
-        lax.fori_loop(0, CX, unpack, 0)
+                beyond = []
+                for a, (above, below) in enumerate(faces):
+                    width = DEPTH - a
+                    shift = width * (CX * j + x)
+                    moved = jnp.where(within(lane, shift, width), above, below)
+                    if shift:
+                        moved = pltpu.roll(moved, LANES - shift, 1)
+                    halo = within(lane, 0, width) | within(lane, LANES - width, width)
+                    beyond.append(jnp.where(halo, moved, 0.0))
+                res[i, TILES, j] = jnp.maximum(beyond[0], NOTHING)
+                rem[i, TILES, j] = 0.5 * beyond[1]
 
     def right(values):
         rolled = [pltpu.roll(v, LANES - 1, 1) for v in values]
@@ -288,8 +299,10 @@
 def correct_kernel(gathered_ref, inverse_ref, support_ref, smooth_ref, out_ref, buf, sems):
     zero = jnp.zeros((CF, LANES), jnp.float32)
     sums = [zero] * 4
-    for q in range(gathered_ref.shape[0]):
-        part = inverse_ref[:, q * LANES : (q + 1) * LANES] * gathered_ref[pl.ds(q, 1), :]
+    count = gathered_ref.shape[0]
+    for q in range(count):
+        row = gathered_ref[pl.ds(turned(q, -TURN_X, count), 1), :]
+        part = inverse_ref[:, q * LANES : (q + 1) * LANES] * row
         sums[q % 4] = sums[q % 4] + part
     total = (sums[0] + sums[1]) + (sums[2] + sums[3])
     column = jnp.broadcast_to(jnp.sum(total, axis=1, keepdims=True), (CF, LANES))
@@ -338,18 +351,21 @@
 
     message, own = call(
         coarse_kernel,
-        [held(n_gy, FACE + STRIP, LANES), held(OWN, LANES)],
-        specs(pltpu.HBM, 3),
-        [residual, support, classes],
+        [held(n_gy, STRIP, LANES), held(OWN, LANES)],
+        specs(pltpu.HBM, 4),
+        [class_perm, residual, support, classes],
         scratch_shapes=[
+            pltpu.SMEM(class_perm.shape, jnp.float32),
             pltpu.VMEM((ROWS, LANES), jnp.int32),
             pltpu.VMEM((ROWS, LANES), jnp.int32),
+            pltpu.SemaphoreType.DMA,
             pltpu.SemaphoreType.DMA((CHUNKS, 3)),
         ],
         limit=60,
         name="coarse",
     )
-    got = lax.all_to_all(message, "gy", 0, 0, tiled=True)
+    columns = [[turned(k, TURN_Y, n_gy) for k in range(n_gy)]]
+    got = lax.all_to_all(message, "gy", 0, 0, axis_index_groups=columns, tiled=True)
     (own,) = call(
         merge_kernel,
         [held(OWN, LANES)],
@@ -365,7 +381,7 @@
     (rows,) = call(
         pair_kernel, [held(n_gx // 2, 2, LANES)], specs(pltpu.VMEM, 2), [own, mate], name="pair"
     )
-    groups = [list(range(k, n_gx, 2)) for k in range(2)]
+    groups = [[turned(2 * i, TURN_X, n_gx) + k for i in range(n_gx // 2)] for k in range(2)]
     gathered = lax.all_to_all(rows, "gx", 0, 0, axis_index_groups=groups, tiled=True)
     gathered = gathered.reshape(n_gx, LANES)
 
@@ -373,8 +389,8 @@
     (smooth,) = call(
         smooth_kernel,
         [held(ROWS, LANES)],
-        specs(pltpu.SMEM) + specs(pltpu.VMEM, 3) + specs(pl.ANY),
-        [class_perm, own, mate, other, rows],
+        specs(pltpu.VMEM, 3) + specs(pl.ANY),
+        [own, mate, other, rows],
         flops=20_000_000,
         scratch_shapes=[planes] * 8
         + [

time: 47.3 us -> 41.8 us (0.88)
  waiting for transfers between devices: 2.7 us -> 0.07 us
  blocking collectives: 18.3 us -> 16.1 us
  Pallas kernels: 9.45 us -> 8.06 us
  starting transfers between devices: 16.5 us -> 17.2 us
    all_to_all x1, waiting for transfers between devices: 2.69 us -> 0.06 us  [local(): lax.all_to_all(rows, 'gx', 0, 0, axis_index_groups=groups, tiled=True)]
    all_to_all x1, blocking collectives: 18.3 us -> 16.1 us  [local(): lax.all_to_all(message, 'gy', 0, 0, axis_index_groups=columns, tiled=True)]
    pallas_call x5, Pallas kernels: 9.45 us -> 8.06 us  [call(): pl.pallas_call(kernel, out_shape=outs, in_specs=ins, out_specs=specs(out_...]
    all_to_all x1, starting transfers between devices: 9.51 us -> 10.6 us  [local(): lax.all_to_all(rows, 'gx', 0, 0, axis_index_groups=groups, tiled=True)]
  transfers between devices with their start and end apart: 3 -> 3, of which waited for: 1 -> 1; matrix products, arithmetic and copies ran while one was open for 0% -> 0% of each run, Pallas kernels for 14% -> 12%
where the time goes in v7:
time: 41.8 us; the launch traced here: 41.5 us
  starting transfers between devices  17.2 us (41%)
  blocking collectives  16.1 us (39%)
  Pallas kernels  8.06 us (19%)
    all_to_all x1, blocking collectives, local(): lax.all_to_all(message, 'gy', 0, 0, axis_index_groups=columns, tiled=True)  16.1 us
    all_to_all x1, starting transfers between devices, local(): lax.all_to_all(rows, 'gx', 0, 0, axis_index_groups=groups, tiled=True)  10.6 us
    pallas_call x5, Pallas kernels, call(): pl.pallas_call(kernel, out_shape=outs, in_specs=ins, out_specs=specs(out_...  8.06 us
    ppermute x1, starting transfers between devices, local(): mate = lax.ppermute(own, 'gx', pairs)  3.64 us
    ppermute x1, starting transfers between devices, local(): other = lax.ppermute(own, 'gx', others)  3.02 us
  transfers between devices with their start and end apart: 3, of which 1 were waited for; matrix products, arithmetic and copies ran while one was open for 0% of the time, Pallas kernels for 12%

profile of v7, /device:TPU:1, one launch (start us, length us, event | category | flops | bytes accessed | tf_op | source)
XLA Modules:
  0.0 41.5 jit_solution(15684283792837950147)
XLA Ops:
  0.0 2.1 %coarse.1 = (f32[8,16,128]{2,1,0:T(8,128)S(1)}, f32[1064,128]{1,0:T(8,128)S(1)}) custom-call(f32[16]{0:T(128)} %perm_ref.1, f32[512,128]{1,0:T(8,128)} %bitcast.24, s32[512,128]{1,0:T(8,128)} %bitcast.21, s32[512,128]{1,0:T(8,128)} %bitcast.25), custom_call_target="tpu_custom_call" | custom-call | bytes 1396800 | tf_op jit(solution)/shard_map/coarse/pallas_call | solution.py:333
  2.1 16.1 %all_to_all.10.got_ref = f32[8,16,128]{2,1,0:T(8,128)S(1)} all-to-all(f32[8,16,128]{2,1,0:T(8,128)S(1)} %get-tuple-element.7), channel_id=1, replica_groups={{4,5,6,7,0,1,2,3},{12,13,14,15,8,9,10,11},{20,21,22,23,16,17,18,19},{28..., dimensions={0} | all-to-all | bytes 131072 | tf_op jit(solution)/shard_map/all_to_all | solution.py:368
  18.1 0.1 merge.1.own_ref
  18.2 3.6 %collective-permute-start = (f32[1064,128]{1,0:T(8,128)S(1)}, f32[1064,128]{1,0:T(8,128)S(1)}, u32[]{:S(2)}, u32[]{:S(2)}) collective-permute-start(f32[1064,128]{1,0:T(8,128)S(1)} %merge.1.own_ref), channel_id=1, source_target_pairs={{0,8},{8,0},{16,24},{24,16},{32,40},{40,32},{48,56},{56,48},{64,72... | collective-permute-start | bytes 1634312 | tf_op jit(solution)/shard_map/ppermute | solution.py:379
  21.9 3.0 %collective-permute-start.1 = (f32[1064,128]{1,0:T(8,128)S(1)}, f32[1064,128]{1,0:T(8,128)S(1)}, u32[]{:S(2)}, u32[]{:S(2)}) collective-permute-start(f32[1064,128]{1,0:T(8,128)S(1)} %merge.1.own_ref), channel_id=1, source_target_pairs={{8,16},{16,8},{24,32},{32,24},{40,48},{48,40},{56,64},{64,56},{72,... | collective-permute-start | bytes 1634312 | tf_op jit(solution)/shard_map/ppermute | solution.py:380
  24.9 0.0 collective-permute-done.mate_ref
  24.9 0.6 %pair.1.after_ref = f32[32,2,128]{2,1,0:T(2,128)} custom-call(f32[1064,128]{1,0:T(8,128)S(1)} %merge.1.own_ref, f32[1064,128]{1,0:T(8,128)S(1)} %collective-permute-done.mate_ref), custom_call_target="tpu_custom_call" | custom-call | bytes 1122304 | tf_op jit(solution)/shard_map/pair/pallas_call | solution.py:333
  25.5 10.6 %all-to-all-start.1 = ((f32[32,2,128]{2,1,0:T(2,128)}), f32[32,2,128]{2,1,0:T(2,128)S(1)}, u32[]{:S(2)}, u32[]{:S(2)}) async-start(f32[32,2,128]{2,1,0:T(2,128)} %pair.1.after_ref), calls=%async_computation.1 | async-start | bytes 65536 | tf_op jit(solution)/shard_map/all_to_all | solution.py:385
  36.1 0.0 copy-start
  36.1 0.0 copy-start.1
  36.1 0.0 collective-permute-done.1.other_ref
  36.1 4.3 %smooth.1.smooth_ref = f32[512,128]{1,0:T(8,128)S(1)} custom-call(f32[1064,128]{1,0:T(8,128)S(1)} %merge.1.own_ref, f32[1064,128]{1,0:T(8,128)S(1)} %collective-permute-done.mate_ref, f32[1064,128]{1,0:T(8,128)S(1)} %collective-permute-done.1.other_ref, f32[32,2,128]{2,1,0:T(2,128)} %pair.1.after_ref), custom_call_target="tpu_custom_call" | custom-call | flops 20000000 | bytes 1929216 | tf_op jit(solution)/shard_map/smooth/pallas_call | solution.py:333
  40.4 0.1 all-to-all-done.1
  40.5 0.0 copy-done
  40.5 0.0 copy-done.1
  40.5 1.0 %correct.1 = f32[512,128]{1,0:T(8,128)} custom-call(f32[64,128]{1,0:T(8,128)S(1)} %bitcast.23, f32[16,8192]{1,0:T(8,128)S(1)} %copy-done.1, s32[512,128]{1,0:T(8,128)S(1)} %bitcast.22, f32[512,128]{1,0:T(8,128)S(1)} %smooth.1.smooth_ref), custom_call_target="tpu_custom_call" | custom-call | bytes 1343488 | tf_op jit(solution)/shard_map/correct/pallas_call | solution.py:333
Async XLA Ops:
  18.2 6.7 %collective-permute-start = (f32[1064,128]{1,0:T(8,128)S(1)}, f32[1064,128]{1,0:T(8,128)S(1)}, u32[]{:S(2)}, u32[]{:S(2)}) collective-permute-start(f32[1064,128]{1,0:T(8,128)S(1)} %merge.1.own_ref), channel_id=1, source_target_pairs={{0,8},{8,0},{16,24},{24,16},{32,40},{40,32},{48,56},{56,48},{64,72... | collective-permute-start | bytes 1634312 | tf_op jit(solution)/shard_map/ppermute | solution.py:379
  21.9 14.3 %collective-permute-start.1 = (f32[1064,128]{1,0:T(8,128)S(1)}, f32[1064,128]{1,0:T(8,128)S(1)}, u32[]{:S(2)}, u32[]{:S(2)}) collective-permute-start(f32[1064,128]{1,0:T(8,128)S(1)} %merge.1.own_ref), channel_id=1, source_target_pairs={{8,16},{16,8},{24,32},{32,24},{40,48},{48,40},{56,64},{64,56},{72,... | collective-permute-start | bytes 1634312 | tf_op jit(solution)/shard_map/ppermute | solution.py:380
  25.5 14.9 %all-to-all-start.1 = ((f32[32,2,128]{2,1,0:T(2,128)}), f32[32,2,128]{2,1,0:T(2,128)S(1)}, u32[]{:S(2)}, u32[]{:S(2)}) async-start(f32[32,2,128]{2,1,0:T(2,128)} %pair.1.after_ref), calls=%async_computation.1 | async-start | bytes 65536 | tf_op jit(solution)/shard_map/all_to_all | solution.py:385
  36.1 4.4 %copy-start = (s32[64,4,256]{2,1,0:T(4,128)S(1)}, s32[64,4,256]{2,1,0:T(4,128)}, u32[]{:S(2)}) copy-start(s32[64,4,256]{2,1,0:T(4,128)} %param.8) | copy-start | bytes 786436
  36.1 4.4 %copy-start.1 = (f32[16,8192]{1,0:T(8,128)S(1)}, f32[16,8192]{1,0:T(8,128)}, u32[]{:S(2)}) copy-start(f32[16,8192]{1,0:T(8,128)} %inverse_ref.1) | copy-start | bytes 1572868

commit v8 on v7

--- a/solution.py
+++ b/solution.py
@@ -22,7 +22,7 @@
 SUMS = 2 * ROWS + 2 * STRIP
 OWN = SUMS + 8
 SPARE = 96
-TURN_Y, TURN_X = 4, 32
+TURN_Y = 4
 CHUNKS = 8
 NOTHING = 1e-30
 
@@ -51,6 +51,10 @@
 
 def turned(place, turn, count):
     return (place + turn + count) % count
+
+
+def pair_order(count):
+    return [4 * ((y + 4) % 8) + 3 - x for y in range(8) for x in range(4)]
 
 
 def pick(entries, index):
@@ -299,9 +303,9 @@
 def correct_kernel(gathered_ref, inverse_ref, support_ref, smooth_ref, out_ref, buf, sems):
     zero = jnp.zeros((CF, LANES), jnp.float32)
     sums = [zero] * 4
-    count = gathered_ref.shape[0]
-    for q in range(count):
-        row = gathered_ref[pl.ds(turned(q, -TURN_X, count), 1), :]
+    order = pair_order(gathered_ref.shape[0] // 2)
+    for q in range(gathered_ref.shape[0]):
+        row = gathered_ref[pl.ds(2 * order.index(q // 2) + q % 2, 1), :]
         part = inverse_ref[:, q * LANES : (q + 1) * LANES] * row
         sums[q % 4] = sums[q % 4] + part
     total = (sums[0] + sums[1]) + (sums[2] + sums[3])
@@ -381,7 +385,7 @@
     (rows,) = call(
         pair_kernel, [held(n_gx // 2, 2, LANES)], specs(pltpu.VMEM, 2), [own, mate], name="pair"
     )
-    groups = [[turned(2 * i, TURN_X, n_gx) + k for i in range(n_gx // 2)] for k in range(2)]
+    groups = [[2 * pair + k for pair in pair_order(n_gx // 2)] for k in range(2)]
     gathered = lax.all_to_all(rows, "gx", 0, 0, axis_index_groups=groups, tiled=True)
     gathered = gathered.reshape(n_gx, LANES)
 

time: 41.8 us -> 41.9 us (level)
  transfers between devices with their start and end apart: 3 -> 3, of which waited for: 1 -> 0; matrix products, arithmetic and copies ran while one was open for 0% -> 0% of each run, Pallas kernels for 12% -> 12%
where the time goes in v8:
time: 41.9 us; the launch traced here: 41.5 us
  starting transfers between devices  17.3 us (41%)
  blocking collectives  16.1 us (38%)
  Pallas kernels  8.06 us (19%)
    all_to_all x1, blocking collectives, local(): lax.all_to_all(message, 'gy', 0, 0, axis_index_groups=columns, tiled=True)  16.1 us
    all_to_all x1, starting transfers between devices, local(): lax.all_to_all(rows, 'gx', 0, 0, axis_index_groups=groups, tiled=True)  10.6 us
    pallas_call x5, Pallas kernels, call(): pl.pallas_call(kernel, out_shape=outs, in_specs=ins, out_specs=specs(out_...  8.06 us
    ppermute x1, starting transfers between devices, local(): mate = lax.ppermute(own, 'gx', pairs)  3.64 us
    ppermute x1, starting transfers between devices, local(): other = lax.ppermute(own, 'gx', others)  3.02 us
  transfers between devices with their start and end apart: 3, of which 0 were waited for; matrix products, arithmetic and copies ran while one was open for 0% of the time, Pallas kernels for 12%

profile of v8, /device:TPU:1, one launch (start us, length us, event | category | flops | bytes accessed | tf_op | source)
XLA Modules:
  0.0 41.5 jit_solution(12533265703069423598)
XLA Ops:
  0.0 2.1 %coarse.1 = (f32[8,16,128]{2,1,0:T(8,128)S(1)}, f32[1064,128]{1,0:T(8,128)S(1)}) custom-call(f32[16]{0:T(128)} %perm_ref.1, f32[512,128]{1,0:T(8,128)} %bitcast.24, s32[512,128]{1,0:T(8,128)} %bitcast.21, s32[512,128]{1,0:T(8,128)} %bitcast.25), custom_call_target="tpu_custom_call" | custom-call | bytes 1396800 | tf_op jit(solution)/shard_map/coarse/pallas_call | solution.py:337
  2.1 16.1 %all_to_all.10.got_ref = f32[8,16,128]{2,1,0:T(8,128)S(1)} all-to-all(f32[8,16,128]{2,1,0:T(8,128)S(1)} %get-tuple-element.7), channel_id=1, replica_groups={{4,5,6,7,0,1,2,3},{12,13,14,15,8,9,10,11},{20,21,22,23,16,17,18,19},{28..., dimensions={0} | all-to-all | bytes 131072 | tf_op jit(solution)/shard_map/all_to_all | solution.py:372
  18.1 0.1 merge.1.own_ref
  18.2 3.6 %collective-permute-start = (f32[1064,128]{1,0:T(8,128)S(1)}, f32[1064,128]{1,0:T(8,128)S(1)}, u32[]{:S(2)}, u32[]{:S(2)}) collective-permute-start(f32[1064,128]{1,0:T(8,128)S(1)} %merge.1.own_ref), channel_id=1, source_target_pairs={{0,8},{8,0},{16,24},{24,16},{32,40},{40,32},{48,56},{56,48},{64,72... | collective-permute-start | bytes 1634312 | tf_op jit(solution)/shard_map/ppermute | solution.py:383
  21.9 3.0 %collective-permute-start.1 = (f32[1064,128]{1,0:T(8,128)S(1)}, f32[1064,128]{1,0:T(8,128)S(1)}, u32[]{:S(2)}, u32[]{:S(2)}) collective-permute-start(f32[1064,128]{1,0:T(8,128)S(1)} %merge.1.own_ref), channel_id=1, source_target_pairs={{8,16},{16,8},{24,32},{32,24},{40,48},{48,40},{56,64},{64,56},{72,... | collective-permute-start | bytes 1634312 | tf_op jit(solution)/shard_map/ppermute | solution.py:384
  24.9 0.0 collective-permute-done.mate_ref
  24.9 0.6 %pair.1.after_ref = f32[32,2,128]{2,1,0:T(2,128)} custom-call(f32[1064,128]{1,0:T(8,128)S(1)} %merge.1.own_ref, f32[1064,128]{1,0:T(8,128)S(1)} %collective-permute-done.mate_ref), custom_call_target="tpu_custom_call" | custom-call | bytes 1122304 | tf_op jit(solution)/shard_map/pair/pallas_call | solution.py:337
  25.5 10.6 %all-to-all-start.1 = ((f32[32,2,128]{2,1,0:T(2,128)}), f32[32,2,128]{2,1,0:T(2,128)S(1)}, u32[]{:S(2)}, u32[]{:S(2)}) async-start(f32[32,2,128]{2,1,0:T(2,128)} %pair.1.after_ref), calls=%async_computation.1 | async-start | bytes 65536 | tf_op jit(solution)/shard_map/all_to_all | solution.py:389
  36.2 0.0 copy-start
  36.2 0.0 copy-start.1
  36.2 0.0 collective-permute-done.1.other_ref
  36.2 4.3 %smooth.1.smooth_ref = f32[512,128]{1,0:T(8,128)S(1)} custom-call(f32[1064,128]{1,0:T(8,128)S(1)} %merge.1.own_ref, f32[1064,128]{1,0:T(8,128)S(1)} %collective-permute-done.mate_ref, f32[1064,128]{1,0:T(8,128)S(1)} %collective-permute-done.1.other_ref, f32[32,2,128]{2,1,0:T(2,128)} %pair.1.after_ref), custom_call_target="tpu_custom_call" | custom-call | flops 20000000 | bytes 1929216 | tf_op jit(solution)/shard_map/smooth/pallas_call | solution.py:337
  40.5 0.0 all-to-all-done.1
  40.5 0.0 copy-done
  40.5 0.0 copy-done.1
  40.5 1.0 %correct.1 = f32[512,128]{1,0:T(8,128)} custom-call(f32[64,128]{1,0:T(8,128)S(1)} %bitcast.23, f32[16,8192]{1,0:T(8,128)S(1)} %copy-done.1, s32[512,128]{1,0:T(8,128)S(1)} %bitcast.22, f32[512,128]{1,0:T(8,128)S(1)} %smooth.1.smooth_ref), custom_call_target="tpu_custom_call" | custom-call | bytes 1343488 | tf_op jit(solution)/shard_map/correct/pallas_call | solution.py:337
Async XLA Ops:
  18.2 6.7 %collective-permute-start = (f32[1064,128]{1,0:T(8,128)S(1)}, f32[1064,128]{1,0:T(8,128)S(1)}, u32[]{:S(2)}, u32[]{:S(2)}) collective-permute-start(f32[1064,128]{1,0:T(8,128)S(1)} %merge.1.own_ref), channel_id=1, source_target_pairs={{0,8},{8,0},{16,24},{24,16},{32,40},{40,32},{48,56},{56,48},{64,72... | collective-permute-start | bytes 1634312 | tf_op jit(solution)/shard_map/ppermute | solution.py:383
  21.9 14.4 %collective-permute-start.1 = (f32[1064,128]{1,0:T(8,128)S(1)}, f32[1064,128]{1,0:T(8,128)S(1)}, u32[]{:S(2)}, u32[]{:S(2)}) collective-permute-start(f32[1064,128]{1,0:T(8,128)S(1)} %merge.1.own_ref), channel_id=1, source_target_pairs={{8,16},{16,8},{24,32},{32,24},{40,48},{48,40},{56,64},{64,56},{72,... | collective-permute-start | bytes 1634312 | tf_op jit(solution)/shard_map/ppermute | solution.py:384
  25.5 15.0 %all-to-all-start.1 = ((f32[32,2,128]{2,1,0:T(2,128)}), f32[32,2,128]{2,1,0:T(2,128)S(1)}, u32[]{:S(2)}, u32[]{:S(2)}) async-start(f32[32,2,128]{2,1,0:T(2,128)} %pair.1.after_ref), calls=%async_computation.1 | async-start | bytes 65536 | tf_op jit(solution)/shard_map/all_to_all | solution.py:389
  36.2 4.3 %copy-start = (s32[64,4,256]{2,1,0:T(4,128)S(1)}, s32[64,4,256]{2,1,0:T(4,128)}, u32[]{:S(2)}) copy-start(s32[64,4,256]{2,1,0:T(4,128)} %param.8) | copy-start | bytes 786436
  36.2 4.3 %copy-start.1 = (f32[16,8192]{1,0:T(8,128)S(1)}, f32[16,8192]{1,0:T(8,128)}, u32[]{:S(2)}) copy-start(f32[16,8192]{1,0:T(8,128)} %inverse_ref.1) | copy-start | bytes 1572868
